TPU v7x, 256 devices: a whole 4x4x8 slice. The times are simulated.
256 devices in a mesh: gx: 8 (over x, core), gy: 32 (over z, y).
Axes of the slice: x: 4, y: 4, z: 8, core: 2. Of those that a mesh axis runs over, the one named last changes fastest.
Arguments:
- old_basis: float32 [64, 256, 16384], P(None, 'gx', 'gy'), may hold values from -6 to 6
- new_block: float32 [32, 256, 16384], P(None, 'gx', 'gy'), may hold values from -640 to 640
- source_matrix: float32 [32, 256, 16384], P(None, 'gx', 'gy'), may hold values from -82 to 82
- region_map: int32 [256, 16384], P('gx', 'gy'), may hold values from 0 to 7
- conductivity: float32 [8], replicated, may hold values from 0.1 to 1
- damping: float32 [8], replicated, may hold values from 0.2 to 2
- drift_speed: float32 [8], replicated, may hold values from 0.2 to 2
- heat_capacity: float32 [8], replicated, may hold values from 0.5 to 2
- sensor_cells: int32 [16], replicated, may hold values from 0 to 4194303
Outputs:
- new_basis: float32 [32, 256, 16384], P(None, 'gx', 'gy')
- applied_block: float32 [32, 256, 16384], P(None, 'gx', 'gy')
- stiff_block: float32 [96, 32], replicated
- stiff_row: float32 [32, 64], replicated
- capacity_block: float32 [96, 32], replicated
- sensor_block: float32 [16, 32], replicated
- source_block: float32 [32, 32], replicated
All inputs are finite; a program needn't handle non-finite values.
Results may differ from a plain program's by a relative error of at most 0.0003.
Values sent between devices are 32-bit elements; how exact they have to be, the bound alone decides.
No kernel may reach another device: no remote copies, remote signals or barrier semaphores. Data moves between devices by JAX's collectives and lax.ppermute only.
A program may use at most 128 MiB of HBM per device.

v0:
```python
import jax
import jax.numpy as jnp
from jax import lax
from jax.sharding import PartitionSpec as P

NZ = 64


PRECISE = lax.Precision.HIGHEST


def extended(block, sides, width):
    for axis, dim in sides:
        count = lax.axis_size(axis)
        forward = [(i, i + 1) for i in range(count - 1)]
        backward = [(target, source) for source, target in forward]
        low = lax.ppermute(
            lax.slice_in_dim(block, block.shape[dim] - width, None, axis=dim), axis, forward
        )
        high = lax.ppermute(lax.slice_in_dim(block, 0, width, axis=dim), axis, backward)
        block = jnp.concatenate([low, block, high], axis=dim)
    return block


def contract(left_side, right_side):
    return jnp.einsum("acd,bcd->ab", left_side, right_side, precision=PRECISE)


def combine(weights, fields):
    return jnp.einsum("ab,bcd->acd", weights, fields, precision=PRECISE)


def lower_inverse(gram_matrix):
    factor = jnp.linalg.cholesky(gram_matrix)
    identity = jnp.eye(gram_matrix.shape[0], dtype=gram_matrix.dtype)
    return jax.scipy.linalg.solve_triangular(factor, identity, lower=True)


def diffusion(vectors, near_vectors, near_conduct, conduct):
    summed = jnp.zeros_like(vectors)
    for near_vector, near_coef in zip(near_vectors, near_conduct):
        summed = summed + 0.5 * (conduct + near_coef) * (near_vector - vectors)
    return summed


def per_device(
    old_basis,
    new_block,
    source_matrix,
    region_map,
    conductivity,
    damping,
    drift_speed,
    heat_capacity,
    sensor_cells,
):
    width_x = old_basis.shape[1]
    width_yz = old_basis.shape[2]
    count_x = lax.axis_size("gx")
    count_y = lax.axis_size("gy")
    volume = 1.0 / (width_x * count_x * width_yz * count_y)
    levels = jnp.arange(conductivity.shape[0], dtype=jnp.int32)
    one_hot = (region_map[None] == levels[:, None, None]).astype(jnp.float32)
    tables = jnp.stack([conductivity, drift_speed, damping * heat_capacity, heat_capacity])
    cellwise = jnp.einsum("tr,rcd->tcd", tables, one_hot, precision=PRECISE)
    conduct = cellwise[0]
    drift_cell = cellwise[1]
    loss_cell = cellwise[2]
    capacity_cell = cellwise[3]
    coefficients = cellwise[:2]
    z_index = jnp.arange(width_yz) % NZ
    low_edge = z_index == 0
    high_edge = z_index == NZ - 1

    def lower_z(vectors):
        return jnp.where(low_edge, 0.0, jnp.roll(vectors, 1, axis=-1))

    def upper_z(vectors):
        return jnp.where(high_edge, 0.0, jnp.roll(vectors, -1, axis=-1))

    def neighbours(vectors, x_padded, y_padded):
        field_x, coef_x = x_padded
        field_y, coef_y = y_padded
        near_vectors = [
            field_x[:, :-2],
            field_x[:, 2:],
            field_y[:, :, : -2 * NZ],
            field_y[:, :, 2 * NZ :],
            lower_z(vectors),
            upper_z(vectors),
        ]
        near_conduct = [
            coef_x[0, :-2],
            coef_x[0, 2:],
            coef_y[0, :, : -2 * NZ],
            coef_y[0, :, 2 * NZ :],
            lower_z(conduct),
            upper_z(conduct),
        ]
        return (near_vectors, near_conduct, coef_x[1, 2:])

    def forward(vectors, near_vectors, near_conduct):
        return (
            diffusion(vectors, near_vectors, near_conduct, conduct)
            - loss_cell * vectors
            - drift_cell * (vectors - near_vectors[0])
        )

    basis_x = (extended(old_basis, (("gx", 1),), 1), extended(coefficients, (("gx", 1),), 1))
    basis_y = (extended(old_basis, (("gy", 2),), NZ), extended(coefficients, (("gy", 2),), NZ))
    basis_near, basis_conduct, unused_next = neighbours(old_basis, basis_x, basis_y)
    applied_basis = forward(old_basis, basis_near, basis_conduct)

    def project(target):
        weights = lax.psum(contract(old_basis, target), ("gx", "gy")) * volume
        return target - jnp.einsum("ab,acd->bcd", weights, old_basis, precision=PRECISE)

    cleaned = project(project(new_block))
    index_x = lax.axis_index("gx")
    index_y = lax.axis_index("gy")
    row_span = width_yz * count_y
    x_global = sensor_cells // row_span
    remainder = sensor_cells % row_span
    inside = (x_global // width_x == index_x) & (remainder // width_yz == index_y)
    position = jnp.where(
        inside, (x_global - index_x * width_x) * width_yz + remainder - index_y * width_yz, 0
    )
    gram_inverse = lower_inverse(lax.psum(contract(cleaned, cleaned), ("gx", "gy")) * volume)
    new_basis = combine(gram_inverse, cleaned)
    cand_x = (extended(new_basis, (("gx", 1),), 1), extended(coefficients, (("gx", 1),), 1))
    cand_y = (extended(new_basis, (("gy", 2),), NZ), extended(coefficients, (("gy", 2),), NZ))
    near_vectors, near_conduct, drift_next = neighbours(new_basis, cand_x, cand_y)
    applied = forward(new_basis, near_vectors, near_conduct)
    massed = capacity_cell * new_basis
    row_term = contract(new_basis, applied_basis)
    picked = jnp.take(new_basis.reshape(new_basis.shape[0], -1), position, axis=1)
    partials = (
        contract(old_basis, applied),
        contract(new_basis, applied),
        contract(old_basis, massed),
        contract(new_basis, massed),
        row_term,
        jnp.where(inside[None, :], picked, 0.0).T,
        contract(new_basis, source_matrix),
    )
    applied_block, partials = (applied, partials)
    summed = lax.psum(
        (partials[0], partials[1], partials[2], partials[3], partials[4], partials[5], partials[6]),
        ("gx", "gy"),
    )
    stiff_block = jnp.concatenate([summed[0], summed[1]], axis=0) * volume
    capacity_block = jnp.concatenate([summed[2], summed[3]], axis=0) * volume
    stiff_row = summed[4] * volume
    sensor_block = summed[5]
    source_block = summed[6] * volume
    return (
        new_basis,
        applied_block,
        stiff_block,
        stiff_row,
        capacity_block,
        sensor_block,
        source_block,
    )


def solution(mesh):
    in_specs = (
        P(None, "gx", "gy"),
        P(None, "gx", "gy"),
        P(None, "gx", "gy"),
        P("gx", "gy"),
        P(),
        P(),
        P(),
        P(),
        P(),
    )
    out_specs = (P(None, "gx", "gy"), P(None, "gx", "gy"), P(), P(), P(), P(), P())
    return jax.shard_map(
        per_device, mesh=mesh, in_specs=in_specs, out_specs=out_specs, check_vma=False
    )
```

profile of v0, /device:TPU:1, one launch (start us, length us, event | category | flops | bytes accessed | tf_op | source)
XLA Modules:
  0.0 494.6 jit_solution(14092704844176741926)
XLA Ops:
  3.4 4.6 collective-permute-start.4
  10.6 3.9 collective-permute-start
  20.2 3.6 collective-permute-start.8
  24.6 8.1 %fusion.118 = (f32[64,32,511]{2,1,0:T(8,128)}, f32[64,32,511]{2,1,0:T(8,128)}) fusion(f32[64,32,512]{2,1,0:T(8,128)} %param.9), kind=kLoop, calls=%fused_computation.176 | loop fusion | bytes 16744448 | tf_op jit(solution)/shard_map/jit(_roll_static)/slice | solution.py:79
  36.5 6.8 %fusion.58 = f32[64,32]{0,1:T(8,128)S(1)} fusion(f32[32,32,512]{2,1,0:T(8,128)S(1)} %copy-done.9, f32[64,32,512]{2,1,0:T(8,128)S(1)} %copy-done.1), kind=kOutput, calls=%fused_computation.72 | convolution fusion | flops 402653184 | bytes 6299648 | tf_op jit(solution)/shard_map/acd,bcd->ab/dot_general | solution.py:26
  43.3 80.9 %psum.70 = f32[64,32]{0,1:T(8,128)S(1)} all-reduce(f32[64,32]{0,1:T(8,128)S(1)} %fusion.58), channel_id=1, replica_groups=mesh['gx'=8,'gy'=32] {'gx','gy'}, use_global_device_ids=true, to_apply=%region_0.1 | all-reduce | flops 2048 | bytes 16384 | tf_op jit(solution)/shard_map/psum | solution.py:115
  124.2 8.5 %copy_subtract_fusion = f32[32,32,512]{2,0,1:T(8,128)S(1)} fusion(f32[32,32,512]{2,1,0:T(8,128)} %param.10, f32[64,32]{0,1:T(8,128)S(1)} %psum.70, f32[64,32,512]{2,1,0:T(8,128)} %param.9), kind=kOutput, calls=%fused_computation.65 | convolution fusion | flops 403179520 | bytes 8396800 | tf_op jit(solution)/shard_map/ab,acd->bcd/dot_general | solution.py:116
  134.1 5.7 %convolution_bitcast_fusion.4 = f32[64,32]{0,1:T(8,128)S(1)} fusion(f32[32,32,512]{2,0,1:T(8,128)S(1)} %copy_subtract_fusion, f32[64,32,512]{2,1,0:T(8,128)S(1)} %copy-done.2), kind=kOutput, calls=%fused_computation.76 | convolution fusion | flops 402653184 | bytes 6299648 | tf_op jit(solution)/shard_map/acd,bcd->ab/dot_general | solution.py:26
  139.8 74.2 %psum.71 = f32[64,32]{0,1:T(8,128)S(1)} all-reduce(f32[64,32]{0,1:T(8,128)S(1)} %convolution_bitcast_fusion.4), channel_id=1, replica_groups=mesh['gx'=8,'gy'=32] {'gx','gy'}, use_global_device_ids=true, to_apply=%region_1.2 | all-reduce | flops 2048 | bytes 16384 | tf_op jit(solution)/shard_map/psum | solution.py:115
  214.0 7.4 %convolution_subtract_fusion = f32[32,32,512]{2,0,1:T(8,128)S(1)} fusion(f32[32,32,512]{2,0,1:T(8,128)} %copy-done.8, f32[64,32]{0,1:T(8,128)S(1)} %psum.71, f32[64,32,512]{2,1,0:T(8,128)} %param.9), kind=kOutput, calls=%fused_computation.66 | convolution fusion | flops 403179520 | bytes 8396800 | tf_op jit(solution)/shard_map/ab,acd->bcd/dot_general | solution.py:116
  224.6 73.3 %psum.72 = f32[32,32]{0,1:T(8,128)S(1)} all-reduce(f32[32,32]{0,1:T(8,128)S(1)} %convolution_bitcast_fusion.2), channel_id=1, replica_groups=mesh['gx'=8,'gy'=32] {'gx','gy'}, use_global_device_ids=true, to_apply=%region_2.3 | all-reduce | flops 1024 | bytes 8192 | tf_op jit(solution)/shard_map/psum | solution.py:128
  297.9 2.9 cholesky.17
  304.9 3.5 fusion.129
  308.3 2.8 fusion.122
  314.2 6.5 %copy.159 = f32[32,32,512]{0,2,1:T(8,128)} copy(f32[32,32,512]{2,0,1:T(8,128)} %copy-done.4) | data formatting | bytes 4194304 | tf_op jit(solution)/shard_map/reshape | solution.py:136
  320.7 8.8 %fusion.55 = f32[64,32]{0,1:T(8,128)} fusion(f32[32,32,512]{2,0,1:T(8,128)} %copy-done.4, f32[32,512]{1,0:T(8,128)S(1)} %bitcast.91, f32[64,32,512]{2,1,0:T(8,128)} %param.9), kind=kOutput, calls=%fused_computation.68 | convolution fusion | flops 403177472 | bytes 6365184 | tf_op jit(solution)/shard_map/acd,bcd->ab/dot_general | solution.py:26
  329.5 2.5 fusion.61
  332.6 5.0 %fusion.52 = f32[32,32]{0,1:T(8,128)} fusion(f32[32,32,512]{2,0,1:T(8,128)} %copy-done.4, f32[32,32,512]{2,1,0:T(8,128)S(1)} %copy-done), kind=kOutput, calls=%fused_computation.67 | convolution fusion | flops 201326592 | bytes 4198400 | tf_op jit(solution)/shard_map/acd,bcd->ab/dot_general | solution.py:26
  337.7 3.9 gather_fusion
  343.1 4.3 copy.149
  348.4 2.6 collective-permute-start.9
  351.1 2.6 collective-permute-start.5
  354.9 3.3 collective-permute-start.1
  363.5 4.3 collective-permute-start.10
  369.6 5.6 %fusion.33 = f32[32,32,512]{2,0,1:T(8,128)S(1)} fusion(f32[32,32,512]{2,0,1:T(8,128)S(1)} %copy-done.6, f32[32,32,64]{2,0,1:T(8,128)S(1)} %collective-permute-done.7, f32[32,32,64]{2,0,1:T(8,128)S(1)} %collective-permute-done.5, f32[32,1,512]{2,0,1:T(8,128)S(1)} %collective-permute-done.3, f32[32,1,512]{2,0,1:T(8,128)S(1)} %collective-permute-done.1, ...), kind=kLoop, calls=%fused_computation.41 | loop fusion | flops 15728640 | bytes 9569280 | tf_op jit(solution)/shard_map/sub | solution.py:104
  375.2 2.5 copy.150
  380.0 6.4 %convolution_bitcast_fusion.3 = f32[64,32]{0,1:T(8,128)} fusion(f32[32,32,512]{2,0,1:T(8,128)S(1)} %fusion.33, f32[64,32,512]{2,1,0:T(8,128)S(1)} %copy-done.3), kind=kOutput, calls=%fused_computation.75 | convolution fusion | flops 402653184 | bytes 6299648 | tf_op jit(solution)/shard_map/acd,bcd->ab/dot_general | solution.py:26
  386.3 3.4 collective-permute-done.10
  389.7 4.2 collective-permute-done.11
  394.9 8.5 %fusion.6 = f32[64,32,512]{2,1,0:T(8,128)S(1)} fusion(f32[64,32,512]{2,1,0:T(8,128)S(1)} %copy-done.3, f32[64,32,64]{2,1,0:T(8,128)} %copy-done.14, f32[64,32,64]{2,1,0:T(8,128)} %copy-done.13, f32[64,1,512]{2,1,0:T(1,128)S(1)} %copy.141, f32[64,1,512]{2,1,0:T(1,128)S(1)} %copy.139, f32[64,32,511]{2,1,0:T(8,128)} %get-tuple-element.46, ...), kind=kLoop, calls=%fused_computation.8 | loop fusion | flops 31457280 | bytes 18613248 | tf_op jit(solution)/shard_map/sub | solution.py:104
  403.5 5.7 %fusion.64 = f32[32,64]{1,0:T(8,128)S(1)} fusion(f32[32,32,512]{2,0,1:T(8,128)S(1)} %copy-done.6, f32[64,32,512]{2,1,0:T(8,128)S(1)} %fusion.6), kind=kOutput, calls=%fused_computation.74 | convolution fusion | flops 402653184 | bytes 6299648 | tf_op jit(solution)/shard_map/acd,bcd->ab/dot_general | solution.py:26
  409.3 82.3 %all-reduce = (f32[32,32]{0,1:T(8,128)S(1)}, f32[64,32]{0,1:T(8,128)S(1)}, f32[32,64]{1,0:T(8,128)S(1)}, f32[32,32]{0,1:T(8,128)S(1)}, f32[64,32]{0,1:T(8,128)S(...) all-reduce(f32[32,32]{0,1:T(8,128)S(1)} %convolution_bitcast_fusion, ...), channel_id=1, replica_groups=mesh['gx'=8,'gy'=32] {'gx','gy'}, use_global_device_ids=true, to_apply=%region_6.7 | all-reduce | flops 9728 | bytes 77824 | tf_op jit(solution)/shard_map/psum | solution.py:147
  (115 shorter events, 44.2 us)
Async XLA Ops:
  0.6 332.0 %copy-start = (f32[32,32,512]{2,1,0:T(8,128)S(1)}, f32[32,32,512]{2,1,0:T(8,128)}, u32[]{:S(2)}) copy-start(f32[32,32,512]{2,1,0:T(8,128)} %param.11) | copy-start | bytes 6291460
  3.4 350.2 %collective-permute-start.4 = (f32[2,32,64]{2,1,0:T(8,128)}, f32[2,32,64]{2,1,0:T(8,128)}, u32[]{:S(2)}, u32[]{:S(2)}) collective-permute-start(f32[2,32,64]{2,1,0:T(8,128)} %copy.169), channel_id=1, source_target_pairs={{0,1},{1,2},{2,3},{3,4},{4,5},{5,6},{6,7},{7,8},{8,9},{9,10},{10,1... | collective-permute-start | bytes 49160 | tf_op jit(solution)/shard_map/ppermute | solution.py:17
  8.7 346.2 %collective-permute-start.6 = (f32[2,32,64]{2,1,0:T(8,128)}, f32[2,32,64]{2,1,0:T(8,128)}, u32[]{:S(2)}, u32[]{:S(2)}) collective-permute-start(f32[2,32,64]{2,1,0:T(8,128)} %copy.170), channel_id=1, source_target_pairs={{1,0},{2,1},{3,2},{4,3},{5,4},{6,5},{7,6},{8,7},{9,8},{10,9},{11,1... | collective-permute-start | bytes 49160 | tf_op jit(solution)/shard_map/ppermute | solution.py:20
  10.6 337.9 %collective-permute-start = (f32[2,1,512]{2,1,0:T(1,128)}, f32[2,1,512]{2,1,0:T(1,128)S(1)}, u32[]{:S(2)}, u32[]{:S(2)}) collective-permute-start(f32[2,1,512]{2,1,0:T(1,128)} %copy.166), channel_id=1, source_target_pairs={{0,32},{32,64},{64,96},{96,128},{128,160},{160,192},{192,224},{1,3... | collective-permute-start | bytes 12296 | tf_op jit(solution)/shard_map/ppermute | solution.py:17
  15.1 335.9 %collective-permute-start.2 = (f32[2,1,512]{2,1,0:T(1,128)}, f32[2,1,512]{2,1,0:T(1,128)}, u32[]{:S(2)}, u32[]{:S(2)}) collective-permute-start(f32[2,1,512]{2,1,0:T(1,128)} %copy.168), channel_id=1, source_target_pairs={{32,0},{64,32},{96,64},{128,96},{160,128},{192,160},{224,192},{33,... | collective-permute-start | bytes 12296 | tf_op jit(solution)/shard_map/ppermute | solution.py:20
  20.2 339.2 %collective-permute-start.8 = (f32[64,1,512]{2,0,1:T(8,128)}, f32[64,1,512]{2,0,1:T(8,128)}, u32[]{:S(2)}, u32[]{:S(2)}) collective-permute-start(f32[64,1,512]{2,0,1:T(8,128)} %copy.207), channel_id=1, source_target_pairs={{0,32},{32,64},{64,96},{96,128},{128,160},{160,192},{192,224},{1,3... | collective-permute-start | bytes 393224 | tf_op jit(solution)/shard_map/ppermute | solution.py:17
  24.6 8.2 %copy-start.1 = (f32[64,32,512]{2,1,0:T(8,128)S(1)}, f32[64,32,512]{2,1,0:T(8,128)}, u32[]{:S(2)}) copy-start(f32[64,32,512]{2,1,0:T(8,128)} %param.9) | copy-start | bytes 12582916
  124.2 9.8 %copy-start.2 = (f32[64,32,512]{2,1,0:T(8,128)S(1)}, f32[64,32,512]{2,1,0:T(8,128)}, u32[]{:S(2)}) copy-start(f32[64,32,512]{2,1,0:T(8,128)} %param.9) | copy-start | bytes 12582916
  308.3 5.3 %copy-start.4 = (f32[32,32,512]{2,0,1:T(8,128)}, f32[32,32,512]{2,0,1:T(8,128)S(1)}, u32[]{:S(2)}) copy-start(f32[32,32,512]{2,0,1:T(8,128)S(1)} %fusion.129) | copy-start | bytes 6291460
  320.7 8.8 %copy-start.5 = (f32[32,32,512]{2,0,1:T(8,128)S(1)}, f32[32,32,512]{2,0,1:T(8,128)}, u32[]{:S(2)}) copy-start(f32[32,32,512]{2,0,1:T(8,128)} %copy-done.4) | copy-start | bytes 6291460
  332.6 5.0 %copy-start.15 = (f32[1,32,512]{2,0,1:T(1,128)S(1)}, f32[1,32,512]{2,0,1:T(1,128)}, u32[]{:S(2)}) copy-start(f32[1,32,512]{2,0,1:T(1,128)} %get-tuple-element.63) | copy-start | bytes 196612
  332.6 5.0 %copy-start.16 = (f32[1,32,512]{2,0,1:T(1,128)S(1)}, f32[1,32,512]{2,0,1:T(1,128)}, u32[]{:S(2)}) copy-start(f32[1,32,512]{2,0,1:T(1,128)} %get-tuple-element.64) | copy-start | bytes 196612
  343.0 26.6 %copy-start.22 = (pred[512]{0:T(512)(128)(4,1)}, pred[512]{0:T(512)(128)(4,1)S(1)}, u32[]{:S(2)}) copy-start(pred[512]{0:T(512)(128)(4,1)S(1)} %get-tuple-element.82) | copy-start | bytes 1540
  343.0 26.6 %copy-start.24 = (pred[512]{0:T(512)(128)(4,1)}, pred[512]{0:T(512)(128)(4,1)S(1)}, u32[]{:S(2)}) copy-start(pred[512]{0:T(512)(128)(4,1)S(1)} %get-tuple-element.83) | copy-start | bytes 1540
  343.0 26.6 %copy-start.12 = (f32[32,32,1]{2,0,1:T(8,128)S(1)}, f32[32,32,1]{2,0,1:T(8,128)}, u32[]{:S(2)}) copy-start(f32[32,32,1]{2,0,1:T(8,128)} %get-tuple-element.55) | copy-start | bytes 12292
  343.0 26.5 %copy-start.10 = (f32[32,32,511]{2,0,1:T(8,128)S(1)}, f32[32,32,511]{2,0,1:T(8,128)}, u32[]{:S(2)}) copy-start(f32[32,32,511]{2,0,1:T(8,128)} %get-tuple-element.53) | copy-start | bytes 6279172
  343.1 26.5 %copy-start.11 = (f32[32,32,511]{2,0,1:T(8,128)S(1)}, f32[32,32,511]{2,0,1:T(8,128)}, u32[]{:S(2)}) copy-start(f32[32,32,511]{2,0,1:T(8,128)} %get-tuple-element.54) | copy-start | bytes 6279172
  347.3 22.2 %copy-start.6 = (f32[32,32,512]{2,0,1:T(8,128)S(1)}, f32[32,32,512]{2,0,1:T(8,128)}, u32[]{:S(2)}) copy-start(f32[32,32,512]{2,0,1:T(8,128)} %copy-done.4) | copy-start | bytes 6291460
  348.4 15.0 %collective-permute-start.9 = (f32[64,1,512]{2,0,1:T(8,128)S(1)}, f32[64,1,512]{2,0,1:T(8,128)S(1)}, u32[]{:S(2)}, u32[]{:S(2)}) collective-permute-start(f32[64,1,512]{2,0,1:T(8,128)S(1)} %copy.206), channel_id=1, source_target_pairs={{32,0},{64,32},{96,64},{128,96},{160,128},{192,160},{224,192},{33,... | collective-permute-start | bytes 393224 | tf_op jit(solution)/shard_map/ppermute | solution.py:20
  351.1 18.2 %collective-permute-start.5 = (f32[32,32,64]{2,0,1:T(8,128)}, f32[32,32,64]{2,0,1:T(8,128)S(1)}, u32[]{:S(2)}, u32[]{:S(2)}) collective-permute-start(f32[32,32,64]{2,0,1:T(8,128)} %get-tuple-element.59), channel_id=1, source_target_pairs={{0,1},{1,2},{2,3},{3,4},{4,5},{5,6},{6,7},{7,8},{8,9},{9,10},{10,1... | collective-permute-start | bytes 786440 | tf_op jit(solution)/shard_map/ppermute | solution.py:17
  353.6 15.9 %collective-permute-start.7 = (f32[32,32,64]{2,0,1:T(8,128)}, f32[32,32,64]{2,0,1:T(8,128)S(1)}, u32[]{:S(2)}, u32[]{:S(2)}) collective-permute-start(f32[32,32,64]{2,0,1:T(8,128)} %get-tuple-element.60), channel_id=1, source_target_pairs={{1,0},{2,1},{3,2},{4,3},{5,4},{6,5},{7,6},{8,7},{9,8},{10,9},{11,1... | collective-permute-start | bytes 786440 | tf_op jit(solution)/shard_map/ppermute | solution.py:20
  354.9 13.0 %collective-permute-start.1 = (f32[32,1,512]{2,0,1:T(8,128)}, f32[32,1,512]{2,0,1:T(8,128)S(1)}, u32[]{:S(2)}, u32[]{:S(2)}) collective-permute-start(f32[32,1,512]{2,0,1:T(8,128)} %get-tuple-element.57), channel_id=1, source_target_pairs={{0,32},{32,64},{64,96},{96,128},{128,160},{160,192},{192,224},{1,3... | collective-permute-start | bytes 196616 | tf_op jit(solution)/shard_map/ppermute | solution.py:17
  359.3 9.9 %collective-permute-start.3 = (f32[32,1,512]{2,0,1:T(8,128)}, f32[32,1,512]{2,0,1:T(8,128)S(1)}, u32[]{:S(2)}, u32[]{:S(2)}) collective-permute-start(f32[32,1,512]{2,0,1:T(8,128)} %get-tuple-element.58), channel_id=1, source_target_pairs={{32,0},{64,32},{96,64},{128,96},{160,128},{192,160},{224,192},{33,... | collective-permute-start | bytes 196616 | tf_op jit(solution)/shard_map/ppermute | solution.py:20
  363.5 26.2 %collective-permute-start.10 = (f32[64,32,64]{2,1,0:T(8,128)}, f32[64,32,64]{2,1,0:T(8,128)S(1)}, u32[]{:S(2)}, u32[]{:S(2)}) collective-permute-start(f32[64,32,64]{2,1,0:T(8,128)} %get-tuple-element.51), channel_id=1, source_target_pairs={{0,1},{1,2},{2,3},{3,4},{4,5},{5,6},{6,7},{7,8},{8,9},{9,10},{10,1... | collective-permute-start | bytes 1572872 | tf_op jit(solution)/shard_map/ppermute | solution.py:17
  368.0 26.0 %collective-permute-start.11 = (f32[64,32,64]{2,1,0:T(8,128)}, f32[64,32,64]{2,1,0:T(8,128)S(1)}, u32[]{:S(2)}, u32[]{:S(2)}) collective-permute-start(f32[64,32,64]{2,1,0:T(8,128)} %get-tuple-element.52), channel_id=1, source_target_pairs={{1,0},{2,1},{3,2},{4,3},{5,4},{6,5},{7,6},{8,7},{9,8},{10,9},{11,1... | collective-permute-start | bytes 1572872 | tf_op jit(solution)/shard_map/ppermute | solution.py:20
  380.0 14.9 %copy-start.23 = (pred[512]{0:T(512)(128)(4,1)S(1)}, pred[512]{0:T(512)(128)(4,1)}, u32[]{:S(2)}) copy-start(pred[512]{0:T(512)(128)(4,1)} %copy-done.22) | copy-start | bytes 1540
  380.0 14.9 %copy-start.25 = (pred[512]{0:T(512)(128)(4,1)S(1)}, pred[512]{0:T(512)(128)(4,1)}, u32[]{:S(2)}) copy-start(pred[512]{0:T(512)(128)(4,1)} %copy-done.24) | copy-start | bytes 1540
  403.4 5.8 %copy-start.17 = (f32[64,32]{0,1:T(8,128)S(1)}, f32[64,32]{0,1:T(8,128)}, u32[]{:S(2)}) copy-start(f32[64,32]{0,1:T(8,128)} %fusion.55) | copy-start | bytes 24580
  403.4 5.8 %copy-start.18 = (f32[32,32]{0,1:T(8,128)S(1)}, f32[32,32]{0,1:T(8,128)}, u32[]{:S(2)}) copy-start(f32[32,32]{0,1:T(8,128)} %fusion.61) | copy-start | bytes 12292
  403.4 5.8 %copy-start.19 = (f32[32,32]{0,1:T(8,128)S(1)}, f32[32,32]{0,1:T(8,128)}, u32[]{:S(2)}) copy-start(f32[32,32]{0,1:T(8,128)} %fusion.52) | copy-start | bytes 12292
  403.4 5.8 %copy-start.20 = (f32[64,32]{0,1:T(8,128)S(1)}, f32[64,32]{0,1:T(8,128)}, u32[]{:S(2)}) copy-start(f32[64,32]{0,1:T(8,128)} %convolution_bitcast_fusion.3) | copy-start | bytes 24580
  403.5 5.8 %copy-start.21 = (f32[16,32]{1,0:T(8,128)S(1)}, f32[16,32]{1,0:T(8,128)}, u32[]{:S(2)}) copy-start(f32[16,32]{1,0:T(8,128)} %select_select_fusion.1) | copy-start | bytes 6148
  (7 other events, 14.5 us)
where the time goes:
time: 503 us; the launch traced here: 495 us
  blocking collectives  311 us (62%)
  matrix products  65.4 us (13%)
  local copies, waits for them, and re-layouts  48.7 us (10%)
  starting transfers between devices  32.9 us (7%)
  other arithmetic  27.5 us (5%)
  waiting for transfers between devices  7.87 us (2%)
    psum x2, blocking collectives, project(): weights = lax.psum(contract(old_basis, target), ('gx', 'gy')) * volume  155 us
    psum x1, blocking collectives, per_device(): lax.psum((partials[0], partials[1], partials[2], partials[3], partials[4]...  82.3 us
    psum x1, blocking collectives, per_device(): lax.psum(contract(cleaned, cleaned), ('gx', 'gy')) * volume  73.3 us
    dot_general x9, matrix products, contract(): return jnp.einsum('acd,bcd->ab', left_side, right_side, precision=PRECISE)  44.5 us
    ppermute x6, starting transfers between devices, extended(): lax.ppermute(lax.slice_in_dim(block, block.shape[dim] - width, None, axis...  22.4 us
    unnamed x66, local copies, waits for them, and re-layouts  16.3 us
    dot_general x2, matrix products, project(): jnp.einsum('ab,acd->bcd', weights, old_basis, precision=PRECISE)  15.9 us
    sub x2, other arithmetic, forward(): diffusion(vectors, near_vectors, near_conduct, conduct)  14.2 us
  transfers between devices with their start and end apart: 12, of which 3 were waited for; matrix products, arithmetic and copies ran while one was open for 24% of the time, Pallas kernels for 0%

commit v1 on v0

v1 whole, which is shorter than its diff:
```python
import functools

import jax
import jax.numpy as jnp
from jax import lax
from jax.experimental import pallas as pl
from jax.experimental.pallas import tpu as pltpu
from jax.sharding import PartitionSpec as P

NZ = 64
LANES = 128
OLD = 64
NEW = 32
ALL = OLD + NEW
ROWS = 32
CHUNKS = 4
HALF = ROWS // 2
GROUP = 2
PARTS = 3
FACE = ALL + 8
XFACE = ALL + 16
F32 = jnp.float32
BF16 = jnp.bfloat16
HIGH = lax.Precision.HIGHEST
VMEM_LIMIT = 56 * 1024 * 1024


def split(value, count):
    pieces = []
    for _ in range(count):
        piece = value.astype(BF16)
        pieces.append(piece)
        value = value - piece.astype(F32)
    return pieces


def lanes_of(shape):
    return lax.broadcasted_iota(jnp.int32, shape, len(shape) - 1)


def rows_of(shape):
    return lax.broadcasted_iota(jnp.int32, shape, 0)


def field_row(refs, x):
    old_ref, new_ref = refs
    return jnp.concatenate(
        [old_ref[pl.ds(x, OLD, stride=ROWS), :], new_ref[pl.ds(x, NEW, stride=ROWS), :]], axis=0
    )


def lookup(region, table):
    result = jnp.zeros(region.shape, F32)
    for r in range(8):
        result = jnp.where(region == r, table[r], result)
    return result


def cell_fields(region_ref, conductivity, damping, drift_speed, heat_capacity):
    region = region_ref[...]
    conduct = jnp.zeros(region.shape, F32)
    drift = jnp.zeros(region.shape, F32)
    loss = jnp.zeros(region.shape, F32)
    capacity = jnp.zeros(region.shape, F32)
    for r in range(8):
        here = region == r
        conduct = jnp.where(here, conductivity[r], conduct)
        drift = jnp.where(here, drift_speed[r], drift)
        loss = jnp.where(here, damping[r] * heat_capacity[r], loss)
        capacity = jnp.where(here, heat_capacity[r], capacity)
    return conduct, drift, loss, capacity


def z_terms(conduct, z_index):
    low_z = jnp.where(z_index == 0, 0.0, pltpu.roll(conduct, 1, 1))
    high_z = jnp.where(z_index == NZ - 1, 0.0, pltpu.roll(conduct, conduct.shape[1] - 1, 1))
    return 0.5 * (conduct + low_z), 0.5 * (conduct + high_z)


def coef_writer(coef):
    def keep_coef(index, value):
        for j in range(CHUNKS):
            coef[index * CHUNKS + j] = value[:, j * LANES : (j + 1) * LANES]

    return keep_coef


def pack_kernel(
    region_ref, conductivity, damping, drift_speed, heat_capacity, shifts, edges, *refs
):
    old = refs[:CHUNKS]
    new = refs[CHUNKS : 2 * CHUNKS]
    y_top, y_low, x_top, x_low, coef = refs[2 * CHUNKS :]
    width = CHUNKS * LANES
    conduct, drift, loss, capacity = cell_fields(
        region_ref, conductivity, damping, drift_speed, heat_capacity
    )
    low_half = lanes_of((1, LANES)) < NZ
    first = (old[0], new[0])
    last = (old[CHUNKS - 1], new[CHUNKS - 1])

    def tail(rows, value):
        return jnp.broadcast_to(value, (rows, LANES))

    for r in range(HALF):
        near, far = field_row(last, r), field_row(last, r + HALF)
        y_top[r, 0:ALL, :] = jnp.where(low_half, pltpu.roll(near, NZ, 1), far)
        near, far = field_row(first, r), field_row(first, r + HALF)
        y_low[r, 0:ALL, :] = jnp.where(low_half, near, pltpu.roll(far, NZ, 1))
        near = conduct[r : r + 1, width - LANES :]
        far = conduct[r + HALF : r + HALF + 1, width - LANES :]
        y_top[r, ALL:FACE, :] = tail(8, jnp.where(low_half, pltpu.roll(near, NZ, 1), far))
        near = conduct[r : r + 1, :LANES]
        far = conduct[r + HALF : r + HALF + 1, :LANES]
        y_low[r, ALL:FACE, :] = tail(8, jnp.where(low_half, near, pltpu.roll(far, NZ, 1)))
    for j in range(CHUNKS):
        here = slice(j * LANES, (j + 1) * LANES)
        for out, row in ((x_top, ROWS - 1), (x_low, 0)):
            out[j, 0:ALL, :] = field_row((old[j], new[j]), row)
            out[j, ALL : ALL + 8, :] = tail(8, conduct[row : row + 1, here])
            out[j, ALL + 8 : XFACE, :] = tail(8, drift[row : row + 1, here])

    shape = (ROWS, width)
    lane = lanes_of(shape)
    row = rows_of(shape)
    z_index = lane % NZ
    z_down, z_up = z_terms(conduct, z_index)
    half = 0.5 * conduct
    from_low_y = 0.5 * (conduct + pltpu.roll(conduct, NZ, 1))
    from_high_y = 0.5 * (conduct + pltpu.roll(conduct, width - NZ, 1))
    from_low_x = 0.5 * (conduct + pltpu.roll(conduct, 1, 0))
    from_high_x = 0.5 * (conduct + pltpu.roll(conduct, ROWS - 1, 0))
    y_down = jnp.where(lane < NZ, 0.0, from_low_y)
    y_up = jnp.where(lane >= width - NZ, 0.0, from_high_y)
    x_down = jnp.where(row == 0, 0.0, from_low_x)
    x_up = jnp.where(row == ROWS - 1, 0.0, from_high_x)
    pull = jnp.where(row == 0, 0.0, drift)
    x_last = jnp.where(edges[0] == 1, 1.0, 0.0)
    y_last = jnp.where(edges[1] == 1, 1.0, 0.0)
    border = jnp.where(row == ROWS - 1, half * x_last, 0.0) + jnp.where(
        lane >= width - NZ, half * y_last, 0.0
    )
    keep_coef = coef_writer(coef)
    total = z_down + z_up + y_down + y_up + x_down + x_up + pull + loss + border
    keep_coef(0, x_down + pull)
    keep_coef(1, x_up)
    keep_coef(2, y_down)
    keep_coef(3, y_up)
    keep_coef(4, jnp.where(z_index == 0, 0.0, z_down))
    keep_coef(5, jnp.where(z_index == NZ - 1, 0.0, z_up))
    keep_coef(6, shifts[0] - total)
    keep_coef(7, capacity - shifts[1])


def gram_kernel(places, coef, *refs):
    old = refs[:CHUNKS]
    new = refs[CHUNKS : 2 * CHUNKS]
    source = refs[2 * CHUNKS : 3 * CHUNKS]
    out, sensed, first, second = refs[3 * CHUNKS :]
    low_half = lanes_of((1, LANES)) < NZ
    zero_rows = jnp.zeros((LANES - ALL, first.shape[1]), BF16)
    for stack in (first, second):
        stack[ALL:LANES, :] = zero_rows
        stack[LANES + ALL : 2 * LANES, :] = zero_rows

    def fill(stack, group):
        for r in range(GROUP):
            x = group * GROUP + r
            below = jnp.maximum(x - 1, 0)
            above = jnp.minimum(x + 1, ROWS - 1)
            mid = [field_row((old[j], new[j]), x) for j in range(CHUNKS)]
            swapped = [pltpu.roll(value, NZ, 1) for value in mid]
            for j in range(CHUNKS):
                here = pl.ds(j * LANES, LANES)
                refs_j = (old[j], new[j])
                left = jnp.where(low_half, swapped[max(j - 1, 0)], swapped[j])
                right = jnp.where(low_half, swapped[j], swapped[min(j + 1, CHUNKS - 1)])

                def scale(index):
                    return coef[index * CHUNKS + j, pl.ds(x, 1), :]

                value = mid[j]
                moved = (
                    scale(0) * field_row(refs_j, below)
                    + scale(1) * field_row(refs_j, above)
                    + scale(2) * left
                    + scale(3) * right
                    + scale(4) * pltpu.roll(value, 1, 1)
                    + scale(5) * pltpu.roll(value, LANES - 1, 1)
                    + scale(6) * value
                )
                at = pl.ds((r * CHUNKS + j) * LANES, LANES)
                high, low = split(value, 2)
                stack[0:ALL, at] = high
                stack[LANES : LANES + ALL, at] = low
                base = 2 * LANES
                for item in (moved, scale(7) * value):
                    high, low = split(item, 2)
                    stack[base : base + ALL, at] = high
                    stack[base + ALL : base + 2 * ALL, at] = low
                    base += 2 * ALL
                high, low = split(source[j][pl.ds(x, NEW, stride=ROWS), :], 2)
                stack[base : base + NEW, at] = high
                stack[base + NEW : base + 2 * NEW, at] = low

    def add(stack):
        out[...] += lax.dot_general(
            stack[...],
            stack[0 : 2 * LANES, :],
            (((1,), (1,)), ((), ())),
            preferred_element_type=F32,
        )

    out[...] = jnp.zeros(out.shape, F32)
    groups = ROWS // GROUP
    fill(first, 0)

    def step(i, carry):
        fill(second, 2 * i + 1)
        add(first)
        fill(first, jnp.minimum(2 * i + 2, groups - 1))
        add(second)
        return carry

    lax.fori_loop(0, groups // 2, step, 0)

    lane = lanes_of((ALL, LANES))

    def sense(p, total):
        place = places[p]
        inside = place >= 0
        place = jnp.maximum(place, 0)
        x = place // (CHUNKS * LANES)
        column = place % (CHUNKS * LANES)
        found = jnp.zeros((ALL, LANES), F32)
        for j in range(CHUNKS):
            hit = (lane == column - j * LANES) & inside
            found = jnp.where(hit, field_row((old[j], new[j]), x), found)
        return jnp.where(lane == p, jnp.sum(found, axis=1, keepdims=True), total)

    sensed[...] = lax.fori_loop(0, places.shape[0], sense, jnp.zeros((ALL, LANES), F32))


def fold(block, rows):
    return (
        block[0:rows, 0:LANES]
        + block[rows : 2 * rows, 0:LANES]
        + (block[0:rows, LANES:] + block[rows : 2 * rows, LANES:])
    )


def face_kernel(gram, sensed, y_own, y_near, x_own, x_near, out, diffs, scaled):
    tiles = HALF + CHUNKS
    zero_rows = jnp.zeros((LANES - ALL, tiles * LANES), BF16)
    scaled[ALL:LANES, :] = zero_rows
    scaled[LANES + ALL : 2 * LANES, :] = zero_rows
    for t in range(tiles):
        at = pl.ds(t * LANES, LANES)
        if t < HALF:
            own, near = y_own.at[t], y_near.at[t]
        else:
            own, near = x_own.at[t - HALF], x_near.at[t - HALF]
        value = own[0:ALL, :]
        diff = value - near[0:ALL, :]
        edge = 0.5 * (own[ALL : ALL + 1, :] + near[ALL : ALL + 1, :])
        weighted = edge * diff
        if t >= HALF:
            weighted = weighted + own[ALL + 8 : ALL + 9, :] * value
        high, low = split(diff, 2)
        diffs[0:ALL, at] = high
        diffs[ALL : 2 * ALL, at] = low
        high, low = split(weighted, 2)
        scaled[0:ALL, at] = high
        scaled[LANES : LANES + ALL, at] = low
    faces = lax.dot_general(
        diffs[...], scaled[...], (((1,), (1,)), ((), ())), preferred_element_type=F32
    )
    base = 2 * LANES
    overlap = (
        gram[0:ALL, 0:LANES]
        + gram[0:ALL, LANES:]
        + (gram[LANES : LANES + ALL, 0:LANES] + gram[LANES : LANES + ALL, LANES:])
    )
    moved = fold(gram[base : base + 2 * ALL, :], ALL) - fold(faces, ALL)
    base += 2 * ALL
    massed = fold(gram[base : base + 2 * ALL, :], ALL)
    base += 2 * ALL
    source = fold(gram[base : base + 2 * NEW, :], NEW)
    source = jnp.concatenate([source, jnp.zeros((LANES - NEW, LANES), F32)], axis=0).T
    source = pltpu.roll(source[0:ALL, :], ALL, 1)
    lane = lanes_of((ALL, LANES))
    row = rows_of((ALL, LANES))
    diagonal = jnp.sum(jnp.where(lane == row, massed, 0.0), axis=1, keepdims=True)
    upper = jnp.where(row >= lane, overlap, massed)
    out[0:ALL, :] = jnp.where(lane < ALL, upper, source)
    extra = jnp.where(lane == ALL + 16, diagonal, pltpu.roll(sensed[...], ALL, 1))
    out[ALL : 2 * ALL, :] = jnp.where(lane < ALL, moved, extra)


def small_dot(left, right):
    return lax.dot_general(
        left, right, (((1,), (0,)), ((), ())), preferred_element_type=F32, precision=HIGH
    )


def flip(block):
    rows, columns = block.shape
    if rows < LANES:
        block = jnp.concatenate([block, jnp.zeros((LANES - rows, columns), F32)], axis=0)
    if columns < LANES:
        block = jnp.concatenate([block, jnp.zeros((LANES, LANES - columns), F32)], axis=1)
    return block.T[0:columns, 0:rows]


def lower_inverse(gram):
    shape = (NEW, LANES)
    lane, row = lanes_of(shape), rows_of(shape)
    work = jnp.concatenate(
        [gram, jnp.zeros((NEW, LANES - NEW), F32)], axis=1
    ) + jnp.where(lane == row + NEW, 1.0, 0.0)
    for k in range(NEW):
        pivot = work[k : k + 1, k : k + 1]
        line = work[k : k + 1, :] / pivot
        factor = jnp.where(row[:, 0:1] > k, work[:, k : k + 1], 0.0)
        work = work - factor * line
    pivots = jnp.sum(jnp.where(lane == row, work, 0.0), axis=1, keepdims=True)
    return (work / jnp.sqrt(pivots))[:, NEW : 2 * NEW]


def basis_kernel(
    volume,
    region_ref,
    conductivity,
    damping,
    drift_speed,
    heat_capacity,
    shifts,
    summed,
    y_before,
    y_after,
    x_before,
    x_after,
    *refs,
):
    old = refs[:CHUNKS]
    new = refs[CHUNKS : 2 * CHUNKS]
    refs = refs[2 * CHUNKS :]
    basis_out, applied_out, stiff_block, stiff_row, capacity_block, sensor_block, source_block = refs[:7]
    coef, field, low_y, high_y, basis, applied, first, second, weights, sems = refs[7:]
    width = CHUNKS * LANES

    lane = lanes_of((ALL, LANES))
    row = rows_of((ALL, LANES))
    top = summed[0:ALL, :] * volume
    bottom = summed[ALL : 2 * ALL, :] * volume
    upper = jnp.where(lane < ALL, top, 0.0)
    low_part = jnp.where(lane <= row, upper, 0.0)
    high_part = jnp.where(lane > row, upper, 0.0)
    diagonal = jnp.where(lane == row, low_part, 0.0)
    overlap = (low_part - diagonal)[:, 0:ALL] + flip(low_part[:, 0:ALL])
    mass_diagonal = jnp.where(lane == row, bottom[:, ALL + 16 : ALL + 17], 0.0)
    massed = (high_part + mass_diagonal)[:, 0:ALL] + flip(high_part[:, 0:ALL])
    moved = flip(bottom[:, 0:ALL])
    source = top[:, ALL:LANES]
    sensed = summed[ALL : 2 * ALL, ALL : ALL + 16]

    old_gram = overlap[0:OLD, 0:OLD]
    first_weights = overlap[0:OLD, OLD:ALL]
    new_gram = overlap[OLD:ALL, OLD:ALL]
    second_weights = first_weights - small_dot(old_gram, first_weights)
    left_over = second_weights - small_dot(old_gram, second_weights)
    both = first_weights + second_weights
    both_t = flip(both)
    gram = new_gram - small_dot(flip(first_weights), both) - small_dot(both_t, left_over)
    inverse = lower_inverse(gram)
    mix = jnp.concatenate([-small_dot(inverse, both_t), inverse], axis=1)
    mix_t = flip(mix)
    mix_wide = jnp.concatenate([mix, jnp.zeros((NEW, LANES - ALL), F32)], axis=1)
    for k, piece in enumerate(split(mix_wide, 3)):
        for s in range(PARTS):
            weights[k * NEW : (k + 1) * NEW, s * LANES : (s + 1) * LANES] = piece

    conduct, drift, loss, capacity = cell_fields(
        region_ref, conductivity, damping, drift_speed, heat_capacity
    )
    shape = (ROWS, width)
    lane = lanes_of(shape)
    row = rows_of(shape)
    z_index = lane % NZ
    z_down, z_up = z_terms(conduct, z_index)
    low_half = lanes_of((1, LANES)) < NZ

    def face_conduct(ref, at_low):
        tile = jnp.concatenate([ref[r, ALL : ALL + 1, :] for r in range(HALF)], axis=0)
        turned = pltpu.roll(tile, NZ, 1)
        pair = [tile, turned] if at_low else [turned, tile]
        return jnp.concatenate(pair, axis=0)

    blank = jnp.zeros((ROWS, width - LANES), F32)
    before = jnp.concatenate([face_conduct(y_before, True), blank], axis=1)
    after = jnp.concatenate([blank, face_conduct(y_after, False)], axis=1)
    near_y = jnp.where(lane < NZ, before, pltpu.roll(conduct, NZ, 1))
    far_y = jnp.where(lane >= width - NZ, after, pltpu.roll(conduct, width - NZ, 1))
    x_line = [
        jnp.concatenate([ref[j, ALL : ALL + 1, :] for j in range(CHUNKS)], axis=1)
        for ref in (x_before, x_after)
    ]
    near_x = jnp.where(row == 0, x_line[0], pltpu.roll(conduct, 1, 0))
    far_x = jnp.where(row == ROWS - 1, x_line[1], pltpu.roll(conduct, ROWS - 1, 0))
    keep_coef = coef_writer(coef)
    y_down, y_up = 0.5 * (conduct + near_y), 0.5 * (conduct + far_y)
    x_down, x_up = 0.5 * (conduct + near_x), 0.5 * (conduct + far_x)
    keep_coef(0, x_down + drift)
    keep_coef(1, x_up)
    keep_coef(2, y_down)
    keep_coef(3, y_up)
    keep_coef(4, jnp.where(z_index == 0, 0.0, z_down))
    keep_coef(5, jnp.where(z_index == NZ - 1, 0.0, z_up))
    keep_coef(6, -(z_down + z_up + y_down + y_up + x_down + x_up + drift + loss))

    zero_rows = jnp.zeros((LANES - ALL, width), BF16)
    for stack in (first, second):
        for s in range(PARTS):
            stack[s * LANES + ALL : (s + 1) * LANES, :] = zero_rows

    def fill(stack, tiles):
        for j, tile in enumerate(tiles):
            for s, piece in enumerate(split(tile, PARTS)):
                stack[s * LANES : s * LANES + ALL, pl.ds(j * LANES, LANES)] = piece

    def product(stack):
        result = jnp.dot(weights[...], stack[...], preferred_element_type=F32)
        return result[0:NEW] + (result[NEW : 2 * NEW] + result[2 * NEW : 3 * NEW])

    def row_tiles(x):
        return [field_row((old[j], new[j]), x) for j in range(CHUNKS)]

    def keep(x, value):
        field[x + 1] = value
        for j in range(CHUNKS):
            basis[j, pl.ds(x, NEW, stride=ROWS), :] = value[:, j * LANES : (j + 1) * LANES]

    fill(first, row_tiles(0))

    def basis_step(i, carry):
        fill(second, row_tiles(2 * i + 1))
        keep(2 * i, product(first))
        fill(first, row_tiles(jnp.minimum(2 * i + 2, ROWS - 1)))
        keep(2 * i + 1, product(second))
        return carry

    lax.fori_loop(0, ROWS // 2, basis_step, 0)
    copies = [
        pltpu.make_async_copy(
            basis.at[j], basis_out.at[:, pl.ds(j * LANES, LANES)], sems.at[j]
        )
        for j in range(CHUNKS)
    ]
    for copy in copies:
        copy.start()

    for ref, place in ((x_before, 0), (x_after, ROWS + 1)):
        fill(first, [ref[j, 0:ALL, :] for j in range(CHUNKS)])
        field[place] = product(first)
    for ref, target, at_low in ((y_before, low_y, True), (y_after, high_y, False)):
        for g in range(HALF // CHUNKS):
            stack = first if g % 2 == 0 else second
            fill(stack, [ref[g * CHUNKS + j, 0:ALL, :] for j in range(CHUNKS)])
            value = product(stack)
            for j in range(CHUNKS):
                tile = value[:, j * LANES : (j + 1) * LANES]
                turned = pltpu.roll(tile, NZ, 1)
                r = g * CHUNKS + j
                target[r] = tile if at_low else turned
                target[r + HALF] = turned if at_low else tile

    def apply_step(x, carry):
        mid = [field[x + 1, :, j * LANES : (j + 1) * LANES] for j in range(CHUNKS)]
        swapped = [pltpu.roll(value, NZ, 1) for value in mid]
        for j in range(CHUNKS):
            here = slice(j * LANES, (j + 1) * LANES)
            before_j = swapped[j - 1] if j > 0 else low_y[x]
            after_j = swapped[j + 1] if j < CHUNKS - 1 else high_y[x]
            left = jnp.where(low_half, before_j, swapped[j])
            right = jnp.where(low_half, swapped[j], after_j)

            def scale(index):
                return coef[index * CHUNKS + j, pl.ds(x, 1), :]

            value = mid[j]
            result = (
                scale(0) * field[x, :, here]
                + scale(1) * field[x + 2, :, here]
                + scale(2) * left
                + scale(3) * right
                + scale(4) * pltpu.roll(value, 1, 1)
                + scale(5) * pltpu.roll(value, LANES - 1, 1)
                + scale(6) * value
            )
            applied[j, pl.ds(x, NEW, stride=ROWS), :] = result
        return carry

    lax.fori_loop(0, ROWS, apply_step, 0)
    more = [
        pltpu.make_async_copy(
            applied.at[j], applied_out.at[:, pl.ds(j * LANES, LANES)], sems.at[CHUNKS + j]
        )
        for j in range(CHUNKS)
    ]
    for copy in more:
        copy.start()

    outside = small_dot(left_over, flip(inverse))
    unit = jnp.where(
        lanes_of((NEW, NEW)) == rows_of((NEW, NEW)), 1.0, 0.0
    )
    columns = small_dot(moved, mix_t)
    stiff_block[0:OLD, :] = columns[0:OLD] - shifts[0] * outside
    stiff_block[OLD:ALL, :] = small_dot(mix, columns) - shifts[0] * unit
    stiff_row[...] = small_dot(mix, moved[:, 0:OLD]) - shifts[0] * flip(outside)
    columns = small_dot(massed, mix_t)
    capacity_block[0:OLD, :] = columns[0:OLD] + shifts[1] * outside
    capacity_block[OLD:ALL, :] = small_dot(mix, columns) + shifts[1] * unit
    sensor_block[...] = flip(small_dot(mix, sensed))
    source_block[...] = small_dot(mix, source)

    for copy in copies + more:
        copy.wait()


def all_sum(block):
    count_x = lax.axis_size("gx")
    count_y = lax.axis_size("gy")
    rows = block.shape[0] // count_x

    def swap(pieces, axis):
        return lax.all_to_all(pieces, axis, 0, 0)

    piece = jnp.sum(swap(block.reshape(count_x, rows, LANES), "gx"), axis=0)
    piece = jnp.sum(
        swap(jnp.broadcast_to(piece[None], (count_y, rows, LANES)), "gy"), axis=0
    )
    whole = swap(jnp.broadcast_to(piece[None], (count_x, rows, LANES)), "gx")
    return whole.reshape(block.shape)


def per_device(
    old_basis,
    new_block,
    source_matrix,
    region_map,
    conductivity,
    damping,
    drift_speed,
    heat_capacity,
    sensor_cells,
):
    width_x = old_basis.shape[1]
    width_yz = old_basis.shape[2]
    count_x = lax.axis_size("gx")
    count_y = lax.axis_size("gy")
    volume = 1.0 / (width_x * count_x * width_yz * count_y)
    index_x = lax.axis_index("gx")
    index_y = lax.axis_index("gy")
    old = old_basis.reshape(OLD * ROWS, width_yz)
    new = new_block.reshape(NEW * ROWS, width_yz)
    source = source_matrix.reshape(NEW * ROWS, width_yz)

    row_span = width_yz * count_y
    x_global = sensor_cells // row_span
    remainder = sensor_cells % row_span
    inside = (x_global // width_x == index_x) & (remainder // width_yz == index_y)
    places = jnp.where(
        inside, (x_global - index_x * width_x) * width_yz + remainder - index_y * width_yz, -1
    )
    shifts = jnp.stack(
        [
            6.0 * jnp.mean(conductivity) + jnp.mean(damping * heat_capacity) + jnp.mean(drift_speed),
            jnp.mean(heat_capacity),
        ]
    )
    edges = jnp.stack([index_x == count_x - 1, index_y == count_y - 1]).astype(jnp.int32)

    whole = pl.BlockSpec(memory_space=pltpu.VMEM)
    scalar = pl.BlockSpec(memory_space=pltpu.SMEM)
    hbm = pl.BlockSpec(memory_space=pl.ANY)
    params = pltpu.CompilerParams(vmem_limit_bytes=VMEM_LIMIT)

    def columns(rows):
        return [
            pl.BlockSpec((rows, LANES), functools.partial(lambda j, *_: (0, j), j))
            for j in range(CHUNKS)
        ]

    def shape(*sizes):
        return jax.ShapeDtypeStruct(sizes, F32)

    fields = [old] * CHUNKS + [new] * CHUNKS
    field_specs = columns(OLD * ROWS) + columns(NEW * ROWS)
    tables = (conductivity, damping, drift_speed, heat_capacity)

    y_top, y_low, x_top, x_low, coef = pl.pallas_call(
        pack_kernel,
        grid=(1,),
        out_shape=[
            shape(HALF, FACE, LANES),
            shape(HALF, FACE, LANES),
            shape(CHUNKS, XFACE, LANES),
            shape(CHUNKS, XFACE, LANES),
            shape(8 * CHUNKS, ROWS, LANES),
        ],
        in_specs=[whole] + [scalar] * 6 + field_specs,
        out_specs=[whole] * 5,
        compiler_params=params,
        name="pack",
    )(region_map, *tables, shifts, edges, *fields)

    def onward(value, axis):
        return lax.ppermute(value, axis, [(i, i + 1) for i in range(lax.axis_size(axis) - 1)])

    def backward(value, axis):
        return lax.ppermute(value, axis, [(i + 1, i) for i in range(lax.axis_size(axis) - 1)])

    y_before = onward(y_top, "gy")
    x_before = onward(x_top, "gx")
    y_after = backward(y_low, "gy")
    x_after = backward(x_low, "gx")

    stack_rows = 2 * LANES + 4 * ALL + 2 * NEW
    stack_width = GROUP * CHUNKS * LANES
    gram, sensed = pl.pallas_call(
        gram_kernel,
        grid=(1,),
        out_shape=[shape(stack_rows, 2 * LANES), shape(ALL, LANES)],
        in_specs=[scalar, whole] + field_specs + columns(NEW * ROWS),
        out_specs=[whole] * 2,
        scratch_shapes=[pltpu.VMEM((stack_rows, stack_width), BF16)] * 2,
        compiler_params=params,
        cost_estimate=pl.CostEstimate(
            flops=2 * stack_rows * 2 * LANES * width_x * width_yz,
            bytes_accessed=(ALL + NEW) * 4 * width_x * width_yz,
            transcendentals=0,
        ),
        name="gram",
    )(places, coef, *fields, *([source] * CHUNKS))

    face_width = (HALF + CHUNKS) * LANES
    partial = pl.pallas_call(
        face_kernel,
        out_shape=shape(2 * ALL, LANES),
        in_specs=[whole] * 6,
        out_specs=whole,
        scratch_shapes=[
            pltpu.VMEM((2 * ALL, face_width), BF16),
            pltpu.VMEM((2 * LANES, face_width), BF16),
        ],
        compiler_params=params,
        name="faces",
    )(gram, sensed, y_low, y_before, x_low, x_before)

    summed = all_sum(partial)

    results = pl.pallas_call(
        functools.partial(basis_kernel, volume),
        grid=(1,),
        out_shape=[
            shape(NEW * ROWS, width_yz),
            shape(NEW * ROWS, width_yz),
            shape(ALL, NEW),
            shape(NEW, OLD),
            shape(ALL, NEW),
            shape(16, NEW),
            shape(NEW, NEW),
        ],
        in_specs=[whole] + [scalar] * 5 + [whole] * 5 + field_specs,
        out_specs=[hbm, hbm] + [whole] * 5,
        scratch_shapes=[
            pltpu.VMEM((7 * CHUNKS, ROWS, LANES), F32),
            pltpu.VMEM((ROWS + 2, NEW, width_yz), F32),
            pltpu.VMEM((ROWS, NEW, LANES), F32),
            pltpu.VMEM((ROWS, NEW, LANES), F32),
            pltpu.VMEM((CHUNKS, NEW * ROWS, LANES), F32),
            pltpu.VMEM((CHUNKS, NEW * ROWS, LANES), F32),
            pltpu.VMEM((PARTS * LANES, width_yz), BF16),
            pltpu.VMEM((PARTS * LANES, width_yz), BF16),
            pltpu.VMEM((3 * NEW, PARTS * LANES), BF16),
            pltpu.SemaphoreType.DMA((2 * CHUNKS,)),
        ],
        compiler_params=params,
        name="basis",
    )(region_map, *tables, shifts, summed, y_before, y_after, x_before, x_after, *fields)
    return (
        results[0].reshape(new_block.shape),
        results[1].reshape(new_block.shape),
        *results[2:],
    )


def solution(mesh):
    in_specs = (
        P(None, "gx", "gy"),
        P(None, "gx", "gy"),
        P(None, "gx", "gy"),
        P("gx", "gy"),
        P(),
        P(),
        P(),
        P(),
        P(),
    )
    out_specs = (P(None, "gx", "gy"), P(None, "gx", "gy"), P(), P(), P(), P(), P())
    return jax.shard_map(
        per_device, mesh=mesh, in_specs=in_specs, out_specs=out_specs, check_vma=False
    )
```

time: 503 us -> 154 us (0.31)
  the two profiles are of different devices: /device:TPU:1 before, /device:TPU:40 now
where the time goes in v1:
time: 154 us
  Pallas kernels  76.8 us (50%)
  waiting for transfers between devices  32.1 us (21%)
  starting transfers between devices  29.8 us (19%)
  local copies, waits for them, and re-layouts  6 us (4%)
  other arithmetic  5.56 us (4%)
  between operations  3.41 us (2%)
    pallas_call x1, Pallas kernels, per_device(): pl.pallas_call(gram_kernel, grid=(1,), out_shape=[shape(stack_rows, 2 * L...  38.4 us
    all_to_all x3, waiting for transfers between devices, swap(): return lax.all_to_all(pieces, axis, 0, 0)  32.1 us
    pallas_call x1, Pallas kernels, per_device(): pl.pallas_call(functools.partial(basis_kernel, volume), grid=(1,), out_sh...  28.9 us
    all_to_all x3, starting transfers between devices, swap(): return lax.all_to_all(pieces, axis, 0, 0)  21.2 us
    pallas_call x1, Pallas kernels, per_device(): pl.pallas_call(pack_kernel, grid=(1,), out_shape=[shape(HALF, FACE, LANES...  6.35 us
    ppermute x2, starting transfers between devices, onward(): lax.ppermute(value, axis, [(i, i + 1) for i in range(lax.axis_size(axis)...  4.94 us
    unnamed x18, local copies, waits for them, and re-layouts  4.58 us
    ppermute x2, starting transfers between devices, backward(): lax.ppermute(value, axis, [(i + 1, i) for i in range(lax.axis_size(axis)...  3.65 us
  transfers between devices with their start and end apart: 7, of which 3 were waited for; matrix products, arithmetic and copies ran while one was open for 1% of the time, Pallas kernels for 25%

profile of v1, /device:TPU:40, one launch (start us, length us, event | category | flops | bytes accessed | tf_op | source)
XLA Modules:
  0.0 153.7 jit_solution(3180233580250952399)
XLA Ops:
  0.6 1.3 reduce_sum.56
  1.9 1.3 reduce_sum.54
  3.8 1.3 multiply_reduce_fusion
  6.4 0.6 add_convert_fusion.edges
  7.7 0.6 pad_maximum_fusion.shifts
  8.2 6.4 %pack.1 = (f32[16,104,128]{2,1,0:T(8,128)}, f32[16,104,128]{2,1,0:T(8,128)}, f32[4,112,128]{2,1,0:T(8,128)}, f32[4,112,128]{2,1,0:T(8,128)}, f32[32,32,128]{2,1,0:T(8,128)}) custom-call(s32[32,512]{1,0:T(8,128)} %region_ref.3, f32[8]{0:T(128)} %conductivity.3, f32[8]{0:T(128)} %damping.3, f32[8]{0:T(128)} %drift_speed.3, f32[8]{0:T(128)} %heat_capacity.3, ...), custom_call_target="tpu_custom_call" | custom-call | tf_op jit(solution)/shard_map/pack/pallas_call | solution.py:602
  14.6 3.5 %collective-permute-start = (f32[16,104,128]{2,1,0:T(8,128)}, f32[16,104,128]{2,1,0:T(8,128)S(1)}, u32[]{:S(2)}, u32[]{:S(2)}) collective-permute-start(f32[16,104,128]{2,1,0:T(8,128)} %get-tuple-element.25), channel_id=1, source_target_pairs={{0,1},{1,2},{2,3},{3,4},{4,5},{5,6},{6,7},{7,8},{8,9},{9,10},{10,1... | collective-permute-start | bytes 2555912 | tf_op jit(solution)/shard_map/ppermute | solution.py:619
  18.1 1.5 collective-permute-start.1
  19.6 0.5 and_select_fusion.places
  20.1 38.4 %gram.1 = (f32[704,256]{1,0:T(8,128)}, f32[96,128]{1,0:T(8,128)}) custom-call(s32[16]{0:T(128)} %and_select_fusion.places, f32[32,32,128]{2,1,0:T(8,128)} %get-tuple-element.21.coef, f32[2048,512]{1,0:T(8,128)} %bitcast.15, f32[2048,512]{1,0:T(8,128)} %bitcast.16, f32[2048,512]{1,0:T(8,128)} %bitcast.17, f32[2048,512]{1,0:T(8,128)} %bitcast.18, ...), custom_call_target="tpu_custom_call" | custom-call | flops 5905580032 | bytes 8388608 | tf_op jit(solution)/shard_map/gram/pallas_call | solution.py:631
  58.5 0.0 collective-permute-done.1.x_near.x_before
  58.5 0.0 collective-permute-done.y_near.y_before
  58.5 0.0 copy-start
  58.5 0.7 copy-done.1
  59.2 0.3 copy-done
  59.5 3.2 %faces.1 = f32[192,128]{1,0:T(8,128)} custom-call(f32[704,256]{1,0:T(8,128)} %get-tuple-element.22.gram, f32[96,128]{1,0:T(8,128)} %get-tuple-element.23.sensed, f32[16,104,128]{2,1,0:T(8,128)} %get-tuple-element.24.y_own, f32[16,104,128]{2,1,0:T(8,128)} %copy-done, f32[4,112,128]{2,1,0:T(8,128)} %get-tuple-element.26.x_own, f32[4,112,128]{2,1,0:T(8,128)} %copy-done.1), custom_call_target="tpu_custom_call" | custom-call | tf_op jit(solution)/shard_map/faces/pallas_call | solution.py:648
  62.7 5.7 %all-to-all-start = ((f32[8,24,128]{2,1,0:T(8,128)}), f32[8,24,128]{2,1,0:T(8,128)S(1)}, u32[]{:S(2)}, u32[]{:S(2)}) async-start(f32[8,24,128]{2,1,0:T(8,128)} %bitcast.40), calls=%async_computation | async-start | bytes 196608 | tf_op jit(solution)/shard_map/all_to_all | solution.py:537
  68.4 2.4 %collective-permute-start.2 = (f32[16,104,128]{2,1,0:T(8,128)S(1)}, f32[16,104,128]{2,1,0:T(8,128)S(1)}, u32[]{:S(2)}, u32[]{:S(2)}) collective-permute-start(f32[16,104,128]{2,1,0:T(8,128)S(1)} %copy-done.2), channel_id=1, source_target_pairs={{1,0},{2,1},{3,2},{4,3},{5,4},{6,5},{7,6},{8,7},{9,8},{10,9},{11,1... | collective-permute-start | bytes 2555912 | tf_op jit(solution)/shard_map/ppermute | solution.py:622
  70.7 3.4 %all-to-all-done = f32[8,24,128]{2,1,0:T(8,128)S(1)} async-done(((f32[8,24,128]{2,1,0:T(8,128)}), f32[8,24,128]{2,1,0:T(8,128)S(1)}, u32[]{:S(2)}, u32[]{:S(2)}) %all-to-all-start) | async-done | bytes 98336 | tf_op jit(solution)/shard_map/all_to_all | solution.py:537
  74.2 0.8 broadcast_in_dim.6
  74.9 11.0 %all-to-all-start.1 = ((f32[32,24,128]{2,1,0:T(8,128)}), f32[32,24,128]{2,1,0:T(8,128)S(1)}, u32[]{:S(2)}, u32[]{:S(2)}) async-start(f32[32,24,128]{2,1,0:T(8,128)} %broadcast_in_dim.6), calls=%async_computation.1 | async-start | bytes 786432 | tf_op jit(solution)/shard_map/all_to_all | solution.py:537
  85.9 1.3 collective-permute-start.3
  87.2 22.9 %all-to-all-done.1 = f32[32,24,128]{2,1,0:T(8,128)S(1)} async-done(((f32[32,24,128]{2,1,0:T(8,128)}), f32[32,24,128]{2,1,0:T(8,128)S(1)}, u32[]{:S(2)}, u32[]{:S(2)}) %all-to-all-start.1) | async-done | bytes 393248 | tf_op jit(solution)/shard_map/all_to_all | solution.py:537
  110.2 0.6 broadcast_in_dim.7
  110.8 4.6 %all-to-all-start.2 = ((f32[8,24,128]{2,1,0:T(8,128)}), f32[8,24,128]{2,1,0:T(8,128)S(1)}, u32[]{:S(2)}, u32[]{:S(2)}) async-start(f32[8,24,128]{2,1,0:T(8,128)} %broadcast_in_dim.7), calls=%async_computation.2 | async-start | bytes 196608 | tf_op jit(solution)/shard_map/all_to_all | solution.py:537
  115.4 0.0 collective-permute-done.3.x_after
  115.4 0.0 collective-permute-done.2.y_after
  115.5 5.8 %all-to-all-done.2 = f32[8,24,128]{2,1,0:T(8,128)S(1)} async-done(((f32[8,24,128]{2,1,0:T(8,128)}), f32[8,24,128]{2,1,0:T(8,128)S(1)}, u32[]{:S(2)}, u32[]{:S(2)}) %all-to-all-start.2) | async-done | bytes 98336 | tf_op jit(solution)/shard_map/all_to_all | solution.py:537
  121.2 0.6 copy-done.4
  121.9 28.9 %basis.1 = (f32[1024,512]{1,0:T(8,128)}, f32[1024,512]{1,0:T(8,128)}, f32[96,32]{1,0:T(8,128)}, f32[32,64]{1,0:T(8,128)}, f32[96,32]{1,0:T(8,128)}, /*index=5*/f32[16,32]{1,0:T(8,128)}, f32[32,32]{1,0:T(8,128)}) custom-call(s32[32,512]{1,0:T(8,128)} %region_ref.3, f32[8]{0:T(128)} %conductivity.3, f32[8]{0:T(128)} %damping.3, f32[8]{0:T(128)} %drift_speed.3, ...), custom_call_target="tpu_custom_call" | custom-call | tf_op jit(solution)/shard_map/basis/pallas_call | solution.py:663
  150.8 1.5 copy.18
  152.2 1.5 copy.19
  (14 shorter events, 0.1 us)
Async XLA Ops:
  8.2 11.3 %copy-start.7 = (s32[16]{0:T(128)S(1)}, s32[16]{0:T(128)}, u32[]{:S(2)}) copy-start(s32[16]{0:T(128)} %param.17) | copy-start | bytes 196
  14.6 43.9 %collective-permute-start = (f32[16,104,128]{2,1,0:T(8,128)}, f32[16,104,128]{2,1,0:T(8,128)S(1)}, u32[]{:S(2)}, u32[]{:S(2)}) collective-permute-start(f32[16,104,128]{2,1,0:T(8,128)} %get-tuple-element.25), channel_id=1, source_target_pairs={{0,1},{1,2},{2,3},{3,4},{4,5},{5,6},{6,7},{7,8},{8,9},{9,10},{10,1... | collective-permute-start | bytes 2555912 | tf_op jit(solution)/shard_map/ppermute | solution.py:619
  18.1 40.4 %collective-permute-start.1 = (f32[4,112,128]{2,1,0:T(8,128)}, f32[4,112,128]{2,1,0:T(8,128)S(1)}, u32[]{:S(2)}, u32[]{:S(2)}) collective-permute-start(f32[4,112,128]{2,1,0:T(8,128)} %get-tuple-element.27), channel_id=1, source_target_pairs={{0,32},{32,64},{64,96},{96,128},{128,160},{160,192},{192,224},{1,3... | collective-permute-start | bytes 688136 | tf_op jit(solution)/shard_map/ppermute | solution.py:619
  58.5 9.9 %copy-start.2 = (f32[16,104,128]{2,1,0:T(8,128)S(1)}, f32[16,104,128]{2,1,0:T(8,128)}, u32[]{:S(2)}) copy-start(f32[16,104,128]{2,1,0:T(8,128)} %get-tuple-element.24.y_own) | copy-start | bytes 2555908
  58.5 0.7 copy-start.1
  58.5 1.0 copy-start
  59.5 26.4 %copy-start.6 = (f32[4,112,128]{2,1,0:T(8,128)S(1)}, f32[4,112,128]{2,1,0:T(8,128)}, u32[]{:S(2)}) copy-start(f32[4,112,128]{2,1,0:T(8,128)} %get-tuple-element.26.x_own) | copy-start | bytes 688132
  62.7 11.5 %all-to-all-start = ((f32[8,24,128]{2,1,0:T(8,128)}), f32[8,24,128]{2,1,0:T(8,128)S(1)}, u32[]{:S(2)}, u32[]{:S(2)}) async-start(f32[8,24,128]{2,1,0:T(8,128)} %bitcast.40), calls=%async_computation | async-start | bytes 196608 | tf_op jit(solution)/shard_map/all_to_all | solution.py:537
  68.4 47.1 %collective-permute-start.2 = (f32[16,104,128]{2,1,0:T(8,128)S(1)}, f32[16,104,128]{2,1,0:T(8,128)S(1)}, u32[]{:S(2)}, u32[]{:S(2)}) collective-permute-start(f32[16,104,128]{2,1,0:T(8,128)S(1)} %copy-done.2), channel_id=1, source_target_pairs={{1,0},{2,1},{3,2},{4,3},{5,4},{6,5},{7,6},{8,7},{9,8},{10,9},{11,1... | collective-permute-start | bytes 2555912 | tf_op jit(solution)/shard_map/ppermute | solution.py:622
  74.9 35.2 %all-to-all-start.1 = ((f32[32,24,128]{2,1,0:T(8,128)}), f32[32,24,128]{2,1,0:T(8,128)S(1)}, u32[]{:S(2)}, u32[]{:S(2)}) async-start(f32[32,24,128]{2,1,0:T(8,128)} %broadcast_in_dim.6), calls=%async_computation.1 | async-start | bytes 786432 | tf_op jit(solution)/shard_map/all_to_all | solution.py:537
  85.9 29.5 %collective-permute-start.3 = (f32[4,112,128]{2,1,0:T(8,128)S(1)}, f32[4,112,128]{2,1,0:T(8,128)S(1)}, u32[]{:S(2)}, u32[]{:S(2)}) collective-permute-start(f32[4,112,128]{2,1,0:T(8,128)S(1)} %copy-done.6), channel_id=1, source_target_pairs={{32,0},{64,32},{96,64},{128,96},{160,128},{192,160},{224,192},{33,... | collective-permute-start | bytes 688136 | tf_op jit(solution)/shard_map/ppermute | solution.py:622
  110.8 10.4 %all-to-all-start.2 = ((f32[8,24,128]{2,1,0:T(8,128)}), f32[8,24,128]{2,1,0:T(8,128)S(1)}, u32[]{:S(2)}, u32[]{:S(2)}) async-start(f32[8,24,128]{2,1,0:T(8,128)} %broadcast_in_dim.7), calls=%async_computation.2 | async-start | bytes 196608 | tf_op jit(solution)/shard_map/all_to_all | solution.py:537
  115.4 5.8 %copy-start.5 = (f32[4,112,128]{2,1,0:T(8,128)}, f32[4,112,128]{2,1,0:T(8,128)S(1)}, u32[]{:S(2)}) copy-start(f32[4,112,128]{2,1,0:T(8,128)S(1)} %collective-permute-done.3.x_after) | copy-start | bytes 688132
  115.5 5.8 %copy-start.3 = (f32[16,104,128]{2,1,0:T(8,128)}, f32[16,104,128]{2,1,0:T(8,128)S(1)}, u32[]{:S(2)}) copy-start(f32[16,104,128]{2,1,0:T(8,128)S(1)} %collective-permute-done.2.y_after) | copy-start | bytes 2555908
  121.2 0.6 copy-start.4

commit v2 on v1

--- a/solution.py
+++ b/solution.py
@@ -15,14 +15,22 @@
 ROWS = 32
 CHUNKS = 4
 HALF = ROWS // 2
-GROUP = 2
+GROUP = 4
 PARTS = 3
 FACE = ALL + 8
 XFACE = ALL + 16
+PAYLOAD = 2 * LANES
+ALONG_X = ("x", "core")
+ALONG_Y = ("z", "y")
 F32 = jnp.float32
 BF16 = jnp.bfloat16
 HIGH = lax.Precision.HIGHEST
 VMEM_LIMIT = 56 * 1024 * 1024
+
+
+def position(axes):
+    slow, fast = axes
+    return lax.axis_index(slow) * lax.axis_size(fast) + lax.axis_index(fast)
 
 
 def split(value, count):
@@ -42,18 +50,26 @@
     return lax.broadcasted_iota(jnp.int32, shape, 0)
 
 
-def field_row(refs, x):
-    old_ref, new_ref = refs
-    return jnp.concatenate(
-        [old_ref[pl.ds(x, OLD, stride=ROWS), :], new_ref[pl.ds(x, NEW, stride=ROWS), :]], axis=0
-    )
-
-
-def lookup(region, table):
-    result = jnp.zeros(region.shape, F32)
-    for r in range(8):
-        result = jnp.where(region == r, table[r], result)
-    return result
+def table_mean(table):
+    total = table[0]
+    for r in range(1, 8):
+        total = total + table[r]
+    return total * 0.125
+
+
+def common_shifts(conductivity, damping, drift_speed, heat_capacity):
+    loss = damping[0] * heat_capacity[0]
+    for r in range(1, 8):
+        loss = loss + damping[r] * heat_capacity[r]
+    stiff = 6.0 * table_mean(conductivity) + table_mean(drift_speed) + loss * 0.125
+    return stiff, table_mean(heat_capacity)
+
+
+def row_copies(old, new, rows, sems, x):
+    return [
+        pltpu.make_async_copy(old.at[:, x, :], rows.at[x, pl.ds(0, OLD), :], sems.at[x]),
+        pltpu.make_async_copy(new.at[:, x, :], rows.at[x, pl.ds(OLD, NEW), :], sems.at[x]),
+    ]
 
 
 def cell_fields(region_ref, conductivity, damping, drift_speed, heat_capacity):
@@ -86,37 +102,71 @@
 
 
 def pack_kernel(
-    region_ref, conductivity, damping, drift_speed, heat_capacity, shifts, edges, *refs
+    region_ref,
+    conductivity,
+    damping,
+    drift_speed,
+    heat_capacity,
+    old,
+    new,
+    old_first,
+    old_last,
+    new_first,
+    new_last,
+    y_top,
+    y_low,
+    x_top,
+    x_low,
+    coef,
+    sems,
 ):
-    old = refs[:CHUNKS]
-    new = refs[CHUNKS : 2 * CHUNKS]
-    y_top, y_low, x_top, x_low, coef = refs[2 * CHUNKS :]
     width = CHUNKS * LANES
+    copies = []
+    for out, row, base in ((x_top, ROWS - 1, 0), (x_low, 0, 2 * CHUNKS)):
+        for j in range(CHUNKS):
+            here = pl.ds(j * LANES, LANES)
+            for field, start, count, shift in ((old, 0, OLD, 0), (new, OLD, NEW, CHUNKS)):
+                copies.append(
+                    pltpu.make_async_copy(
+                        field.at[:, row, here],
+                        out.at[j, pl.ds(start, count), :],
+                        sems.at[base + shift + j],
+                    )
+                )
+    for copy in copies:
+        copy.start()
     conduct, drift, loss, capacity = cell_fields(
         region_ref, conductivity, damping, drift_speed, heat_capacity
     )
     low_half = lanes_of((1, LANES)) < NZ
-    first = (old[0], new[0])
-    last = (old[CHUNKS - 1], new[CHUNKS - 1])
 
     def tail(rows, value):
         return jnp.broadcast_to(value, (rows, LANES))
 
+    def turned(ref, f, x):
+        return jnp.transpose(ref[f : f + 8, x : x + 8, :], (1, 0, 2))
+
+    for first, last, start, count in (
+        (old_first, old_last, 0, OLD),
+        (new_first, new_last, OLD, NEW),
+    ):
+        for f in range(0, count, 8):
+            for x in range(0, HALF, 8):
+                at = (slice(x, x + 8), slice(start + f, start + f + 8), slice(None))
+                near, far = turned(last, f, x), turned(last, f, x + HALF)
+                y_top[at] = jnp.where(low_half[None], pltpu.roll(near, NZ, 2), far)
+                near, far = turned(first, f, x), turned(first, f, x + HALF)
+                y_low[at] = jnp.where(low_half[None], near, pltpu.roll(far, NZ, 2))
+    near, far = conduct[:HALF, width - LANES :], conduct[HALF:, width - LANES :]
+    top_line = jnp.where(low_half, pltpu.roll(near, NZ, 1), far)
+    near, far = conduct[:HALF, :LANES], conduct[HALF:, :LANES]
+    low_line = jnp.where(low_half, near, pltpu.roll(far, NZ, 1))
     for r in range(HALF):
-        near, far = field_row(last, r), field_row(last, r + HALF)
-        y_top[r, 0:ALL, :] = jnp.where(low_half, pltpu.roll(near, NZ, 1), far)
-        near, far = field_row(first, r), field_row(first, r + HALF)
-        y_low[r, 0:ALL, :] = jnp.where(low_half, near, pltpu.roll(far, NZ, 1))
-        near = conduct[r : r + 1, width - LANES :]
-        far = conduct[r + HALF : r + HALF + 1, width - LANES :]
-        y_top[r, ALL:FACE, :] = tail(8, jnp.where(low_half, pltpu.roll(near, NZ, 1), far))
-        near = conduct[r : r + 1, :LANES]
-        far = conduct[r + HALF : r + HALF + 1, :LANES]
-        y_low[r, ALL:FACE, :] = tail(8, jnp.where(low_half, near, pltpu.roll(far, NZ, 1)))
+        y_top[r, ALL:FACE, :] = tail(8, top_line[r : r + 1])
+        y_low[r, ALL:FACE, :] = tail(8, low_line[r : r + 1])
     for j in range(CHUNKS):
         here = slice(j * LANES, (j + 1) * LANES)
         for out, row in ((x_top, ROWS - 1), (x_low, 0)):
-            out[j, 0:ALL, :] = field_row((old[j], new[j]), row)
             out[j, ALL : ALL + 8, :] = tail(8, conduct[row : row + 1, here])
             out[j, ALL + 8 : XFACE, :] = tail(8, drift[row : row + 1, here])
 
@@ -135,8 +185,9 @@
     x_down = jnp.where(row == 0, 0.0, from_low_x)
     x_up = jnp.where(row == ROWS - 1, 0.0, from_high_x)
     pull = jnp.where(row == 0, 0.0, drift)
-    x_last = jnp.where(edges[0] == 1, 1.0, 0.0)
-    y_last = jnp.where(edges[1] == 1, 1.0, 0.0)
+    x_last = jnp.where(position(ALONG_X) == lax.axis_size(ALONG_X) - 1, 1.0, 0.0)
+    y_last = jnp.where(position(ALONG_Y) == lax.axis_size(ALONG_Y) - 1, 1.0, 0.0)
+    shifts = common_shifts(conductivity, damping, drift_speed, heat_capacity)
     border = jnp.where(row == ROWS - 1, half * x_last, 0.0) + jnp.where(
         lane >= width - NZ, half * y_last, 0.0
     )
@@ -150,29 +201,47 @@
     keep_coef(5, jnp.where(z_index == NZ - 1, 0.0, z_up))
     keep_coef(6, shifts[0] - total)
     keep_coef(7, capacity - shifts[1])
-
-
-def gram_kernel(places, coef, *refs):
-    old = refs[:CHUNKS]
-    new = refs[CHUNKS : 2 * CHUNKS]
-    source = refs[2 * CHUNKS : 3 * CHUNKS]
-    out, sensed, first, second = refs[3 * CHUNKS :]
+    for copy in copies:
+        copy.wait()
+
+
+def gram_kernel(sensor_cells, coef, old, new, source, out, sensed, stack, rows, sources, sems):
+    width = CHUNKS * LANES
+
+    def incoming(x):
+        return row_copies(old, new, rows, sems, x) + [
+            pltpu.make_async_copy(source.at[:, x, :], sources.at[x], sems.at[x])
+        ]
+
+    def begin(x, carry):
+        for copy in incoming(x):
+            copy.start()
+        return carry
+
+    lax.fori_loop(0, ROWS, begin, 0)
     low_half = lanes_of((1, LANES)) < NZ
-    zero_rows = jnp.zeros((LANES - ALL, first.shape[1]), BF16)
-    for stack in (first, second):
-        stack[ALL:LANES, :] = zero_rows
-        stack[LANES + ALL : 2 * LANES, :] = zero_rows
-
-    def fill(stack, group):
+    zero_rows = jnp.zeros((LANES - ALL, stack.shape[1]), BF16)
+    stack[ALL:LANES, :] = zero_rows
+    stack[LANES + ALL : 2 * LANES, :] = zero_rows
+    out[...] = jnp.zeros(out.shape, F32)
+
+    def arrive(x):
+        for copy in incoming(x):
+            copy.wait()
+
+    def fill(group):
         for r in range(GROUP):
             x = group * GROUP + r
+            if r < GROUP - 1:
+                arrive(x + 1)
+            else:
+                pl.when(x + 1 < ROWS)(lambda: arrive(x + 1))
             below = jnp.maximum(x - 1, 0)
             above = jnp.minimum(x + 1, ROWS - 1)
-            mid = [field_row((old[j], new[j]), x) for j in range(CHUNKS)]
+            mid = [rows[x, :, j * LANES : (j + 1) * LANES] for j in range(CHUNKS)]
             swapped = [pltpu.roll(value, NZ, 1) for value in mid]
             for j in range(CHUNKS):
-                here = pl.ds(j * LANES, LANES)
-                refs_j = (old[j], new[j])
+                here = slice(j * LANES, (j + 1) * LANES)
                 left = jnp.where(low_half, swapped[max(j - 1, 0)], swapped[j])
                 right = jnp.where(low_half, swapped[j], swapped[min(j + 1, CHUNKS - 1)])
 
@@ -181,8 +250,8 @@
 
                 value = mid[j]
                 moved = (
-                    scale(0) * field_row(refs_j, below)
-                    + scale(1) * field_row(refs_j, above)
+                    scale(0) * rows[below, :, here]
+                    + scale(1) * rows[above, :, here]
                     + scale(2) * left
                     + scale(3) * right
                     + scale(4) * pltpu.roll(value, 1, 1)
@@ -199,46 +268,49 @@
                     stack[base : base + ALL, at] = high
                     stack[base + ALL : base + 2 * ALL, at] = low
                     base += 2 * ALL
-                high, low = split(source[j][pl.ds(x, NEW, stride=ROWS), :], 2)
+                high, low = split(sources[x, :, here], 2)
                 stack[base : base + NEW, at] = high
                 stack[base + NEW : base + 2 * NEW, at] = low
 
-    def add(stack):
+    arrive(0)
+
+    def step(i, carry):
+        fill(i)
         out[...] += lax.dot_general(
             stack[...],
             stack[0 : 2 * LANES, :],
             (((1,), (1,)), ((), ())),
             preferred_element_type=F32,
         )
-
-    out[...] = jnp.zeros(out.shape, F32)
-    groups = ROWS // GROUP
-    fill(first, 0)
-
-    def step(i, carry):
-        fill(second, 2 * i + 1)
-        add(first)
-        fill(first, jnp.minimum(2 * i + 2, groups - 1))
-        add(second)
         return carry
 
-    lax.fori_loop(0, groups // 2, step, 0)
+    lax.fori_loop(0, ROWS // GROUP, step, 0)
 
     lane = lanes_of((ALL, LANES))
-
-    def sense(p, total):
-        place = places[p]
-        inside = place >= 0
-        place = jnp.maximum(place, 0)
-        x = place // (CHUNKS * LANES)
-        column = place % (CHUNKS * LANES)
-        found = jnp.zeros((ALL, LANES), F32)
-        for j in range(CHUNKS):
-            hit = (lane == column - j * LANES) & inside
-            found = jnp.where(hit, field_row((old[j], new[j]), x), found)
-        return jnp.where(lane == p, jnp.sum(found, axis=1, keepdims=True), total)
-
-    sensed[...] = lax.fori_loop(0, places.shape[0], sense, jnp.zeros((ALL, LANES), F32))
+    sensed[...] = jnp.zeros(sensed.shape, F32)
+    row_span = width * lax.axis_size(ALONG_Y)
+    index_x, index_y = position(ALONG_X), position(ALONG_Y)
+
+    def sense(p, carry):
+        cell = sensor_cells[p]
+        x_global = cell // row_span
+        remainder = cell % row_span
+        inside = (x_global // ROWS == index_x) & (remainder // width == index_y)
+
+        @pl.when(inside)
+        def _():
+            x = x_global % ROWS
+            column = remainder % width
+            found = jnp.zeros((ALL, LANES), F32)
+            for j in range(CHUNKS):
+                value = rows[x, :, j * LANES : (j + 1) * LANES]
+                found = jnp.where(lane == column - j * LANES, value, found)
+            picked = jnp.sum(found, axis=1, keepdims=True)
+            sensed[...] = jnp.where(lane == p, picked, sensed[...])
+
+        return carry
+
+    lax.fori_loop(0, sensor_cells.shape[0], sense, 0)
 
 
 def fold(block, rows):
@@ -295,6 +367,7 @@
     out[0:ALL, :] = jnp.where(lane < ALL, upper, source)
     extra = jnp.where(lane == ALL + 16, diagonal, pltpu.roll(sensed[...], ALL, 1))
     out[ALL : 2 * ALL, :] = jnp.where(lane < ALL, moved, extra)
+    out[2 * ALL : PAYLOAD, :] = jnp.zeros((PAYLOAD - 2 * ALL, LANES), F32)
 
 
 def small_dot(left, right):
@@ -334,20 +407,42 @@
     damping,
     drift_speed,
     heat_capacity,
-    shifts,
     summed,
     y_before,
     y_after,
     x_before,
     x_after,
-    *refs,
+    old,
+    new,
+    basis_out,
+    applied_out,
+    stiff_block,
+    stiff_row,
+    capacity_block,
+    sensor_block,
+    source_block,
+    rows,
+    coef,
+    field,
+    applied,
+    low_y,
+    high_y,
+    first,
+    second,
+    weights,
+    sems,
+    basis_sems,
+    applied_sems,
 ):
-    old = refs[:CHUNKS]
-    new = refs[CHUNKS : 2 * CHUNKS]
-    refs = refs[2 * CHUNKS :]
-    basis_out, applied_out, stiff_block, stiff_row, capacity_block, sensor_block, source_block = refs[:7]
-    coef, field, low_y, high_y, basis, applied, first, second, weights, sems = refs[7:]
     width = CHUNKS * LANES
+
+    def begin(x, carry):
+        for copy in row_copies(old, new, rows, sems, x):
+            copy.start()
+        return carry
+
+    lax.fori_loop(0, ROWS, begin, 0)
+    shifts = common_shifts(conductivity, damping, drift_speed, heat_capacity)
 
     lane = lanes_of((ALL, LANES))
     row = rows_of((ALL, LANES))
@@ -432,33 +527,6 @@
         result = jnp.dot(weights[...], stack[...], preferred_element_type=F32)
         return result[0:NEW] + (result[NEW : 2 * NEW] + result[2 * NEW : 3 * NEW])
 
-    def row_tiles(x):
-        return [field_row((old[j], new[j]), x) for j in range(CHUNKS)]
-
-    def keep(x, value):
-        field[x + 1] = value
-        for j in range(CHUNKS):
-            basis[j, pl.ds(x, NEW, stride=ROWS), :] = value[:, j * LANES : (j + 1) * LANES]
-
-    fill(first, row_tiles(0))
-
-    def basis_step(i, carry):
-        fill(second, row_tiles(2 * i + 1))
-        keep(2 * i, product(first))
-        fill(first, row_tiles(jnp.minimum(2 * i + 2, ROWS - 1)))
-        keep(2 * i + 1, product(second))
-        return carry
-
-    lax.fori_loop(0, ROWS // 2, basis_step, 0)
-    copies = [
-        pltpu.make_async_copy(
-            basis.at[j], basis_out.at[:, pl.ds(j * LANES, LANES)], sems.at[j]
-        )
-        for j in range(CHUNKS)
-    ]
-    for copy in copies:
-        copy.start()
-
     for ref, place in ((x_before, 0), (x_after, ROWS + 1)):
         fill(first, [ref[j, 0:ALL, :] for j in range(CHUNKS)])
         field[place] = product(first)
@@ -474,7 +542,22 @@
                 target[r] = tile if at_low else turned
                 target[r + HALF] = turned if at_low else tile
 
-    def apply_step(x, carry):
+    def load(stack, x):
+        for copy in row_copies(old, new, rows, sems, x):
+            copy.wait()
+        fill(stack, [rows[x, :, j * LANES : (j + 1) * LANES] for j in range(CHUNKS)])
+
+    def basis_copy(x):
+        return pltpu.make_async_copy(field.at[x + 1], basis_out.at[:, x, :], basis_sems.at[x])
+
+    def applied_copy(x):
+        return pltpu.make_async_copy(applied.at[x], applied_out.at[:, x, :], applied_sems.at[x])
+
+    def keep(x, stack):
+        field[x + 1] = product(stack)
+        basis_copy(x).start()
+
+    def apply(x):
         mid = [field[x + 1, :, j * LANES : (j + 1) * LANES] for j in range(CHUNKS)]
         swapped = [pltpu.roll(value, NZ, 1) for value in mid]
         for j in range(CHUNKS):
@@ -488,7 +571,7 @@
                 return coef[index * CHUNKS + j, pl.ds(x, 1), :]
 
             value = mid[j]
-            result = (
+            applied[x, :, here] = (
                 scale(0) * field[x, :, here]
                 + scale(1) * field[x + 2, :, here]
                 + scale(2) * left
@@ -497,51 +580,73 @@
                 + scale(5) * pltpu.roll(value, LANES - 1, 1)
                 + scale(6) * value
             )
-            applied[j, pl.ds(x, NEW, stride=ROWS), :] = result
+        applied_copy(x).start()
+
+    load(first, 0)
+    load(second, 1)
+    keep(0, first)
+
+    def step(i, carry):
+        x = 2 * i + 1
+        keep(x, second)
+        load(first, x + 1)
+        apply(x - 1)
+        keep(x + 1, first)
+        load(second, x + 2)
+        apply(x)
         return carry
 
-    lax.fori_loop(0, ROWS, apply_step, 0)
-    more = [
-        pltpu.make_async_copy(
-            applied.at[j], applied_out.at[:, pl.ds(j * LANES, LANES)], sems.at[CHUNKS + j]
-        )
-        for j in range(CHUNKS)
-    ]
-    for copy in more:
-        copy.start()
+    lax.fori_loop(0, ROWS // 2 - 1, step, 0)
+    keep(ROWS - 1, second)
+    apply(ROWS - 2)
+    apply(ROWS - 1)
 
     outside = small_dot(left_over, flip(inverse))
     unit = jnp.where(
         lanes_of((NEW, NEW)) == rows_of((NEW, NEW)), 1.0, 0.0
     )
     columns = small_dot(moved, mix_t)
-    stiff_block[0:OLD, :] = columns[0:OLD] - shifts[0] * outside
-    stiff_block[OLD:ALL, :] = small_dot(mix, columns) - shifts[0] * unit
+    stiff_columns = columns[0:OLD] - shifts[0] * outside
+    stiff_rest = small_dot(mix, columns) - shifts[0] * unit
+    stiff_block[...] = flip(jnp.concatenate([stiff_columns, stiff_rest], axis=0))
     stiff_row[...] = small_dot(mix, moved[:, 0:OLD]) - shifts[0] * flip(outside)
     columns = small_dot(massed, mix_t)
-    capacity_block[0:OLD, :] = columns[0:OLD] + shifts[1] * outside
-    capacity_block[OLD:ALL, :] = small_dot(mix, columns) + shifts[1] * unit
+    mass_columns = columns[0:OLD] + shifts[1] * outside
+    mass_rest = small_dot(mix, columns) + shifts[1] * unit
+    capacity_block[...] = flip(jnp.concatenate([mass_columns, mass_rest], axis=0))
     sensor_block[...] = flip(small_dot(mix, sensed))
     source_block[...] = small_dot(mix, source)
 
-    for copy in copies + more:
-        copy.wait()
+    def finish(x, carry):
+        basis_copy(x).wait()
+        applied_copy(x).wait()
+        return carry
+
+    lax.fori_loop(0, ROWS, finish, 0)
+
+
+def swap(pieces, axes):
+    return lax.all_to_all(pieces, axes, 0, 0)
+
+
+def spread(block, axes):
+    count = lax.axis_size(axes)
+    return jnp.sum(swap(block.reshape(count, -1, LANES), axes), axis=0)
+
+
+def copies_of(piece, axes):
+    return swap(jnp.broadcast_to(piece[None], (lax.axis_size(axes), *piece.shape)), axes)
+
+
+def gathered(piece, axes):
+    return copies_of(piece, axes).reshape(-1, LANES)
 
 
 def all_sum(block):
-    count_x = lax.axis_size("gx")
-    count_y = lax.axis_size("gy")
-    rows = block.shape[0] // count_x
-
-    def swap(pieces, axis):
-        return lax.all_to_all(pieces, axis, 0, 0)
-
-    piece = jnp.sum(swap(block.reshape(count_x, rows, LANES), "gx"), axis=0)
-    piece = jnp.sum(
-        swap(jnp.broadcast_to(piece[None], (count_y, rows, LANES)), "gy"), axis=0
-    )
-    whole = swap(jnp.broadcast_to(piece[None], (count_x, rows, LANES)), "gx")
-    return whole.reshape(block.shape)
+    inner, outer = ("core", "z"), ("x", "y")
+    piece = spread(block, inner)
+    piece = jnp.sum(copies_of(piece, outer), axis=0)
+    return gathered(piece, inner)
 
 
 def per_device(
@@ -557,46 +662,20 @@
 ):
     width_x = old_basis.shape[1]
     width_yz = old_basis.shape[2]
-    count_x = lax.axis_size("gx")
-    count_y = lax.axis_size("gy")
+    count_x = lax.axis_size(ALONG_X)
+    count_y = lax.axis_size(ALONG_Y)
     volume = 1.0 / (width_x * count_x * width_yz * count_y)
-    index_x = lax.axis_index("gx")
-    index_y = lax.axis_index("gy")
-    old = old_basis.reshape(OLD * ROWS, width_yz)
-    new = new_block.reshape(NEW * ROWS, width_yz)
-    source = source_matrix.reshape(NEW * ROWS, width_yz)
-
-    row_span = width_yz * count_y
-    x_global = sensor_cells // row_span
-    remainder = sensor_cells % row_span
-    inside = (x_global // width_x == index_x) & (remainder // width_yz == index_y)
-    places = jnp.where(
-        inside, (x_global - index_x * width_x) * width_yz + remainder - index_y * width_yz, -1
-    )
-    shifts = jnp.stack(
-        [
-            6.0 * jnp.mean(conductivity) + jnp.mean(damping * heat_capacity) + jnp.mean(drift_speed),
-            jnp.mean(heat_capacity),
-        ]
-    )
-    edges = jnp.stack([index_x == count_x - 1, index_y == count_y - 1]).astype(jnp.int32)
-
     whole = pl.BlockSpec(memory_space=pltpu.VMEM)
     scalar = pl.BlockSpec(memory_space=pltpu.SMEM)
     hbm = pl.BlockSpec(memory_space=pl.ANY)
     params = pltpu.CompilerParams(vmem_limit_bytes=VMEM_LIMIT)
 
-    def columns(rows):
-        return [
-            pl.BlockSpec((rows, LANES), functools.partial(lambda j, *_: (0, j), j))
-            for j in range(CHUNKS)
-        ]
-
     def shape(*sizes):
         return jax.ShapeDtypeStruct(sizes, F32)
 
-    fields = [old] * CHUNKS + [new] * CHUNKS
-    field_specs = columns(OLD * ROWS) + columns(NEW * ROWS)
+    def column(count, j):
+        return pl.BlockSpec((count, ROWS, LANES), lambda *_: (0, 0, j))
+
     tables = (conductivity, damping, drift_speed, heat_capacity)
 
     y_top, y_low, x_top, x_low, coef = pl.pallas_call(
@@ -609,11 +688,24 @@
             shape(CHUNKS, XFACE, LANES),
             shape(8 * CHUNKS, ROWS, LANES),
         ],
-        in_specs=[whole] + [scalar] * 6 + field_specs,
+        in_specs=[whole]
+        + [scalar] * 4
+        + [hbm] * 2
+        + [column(OLD, 0), column(OLD, CHUNKS - 1), column(NEW, 0), column(NEW, CHUNKS - 1)],
         out_specs=[whole] * 5,
+        scratch_shapes=[pltpu.SemaphoreType.DMA((4 * CHUNKS,))],
         compiler_params=params,
         name="pack",
-    )(region_map, *tables, shifts, edges, *fields)
+    )(
+        region_map,
+        *tables,
+        old_basis,
+        new_block,
+        old_basis,
+        old_basis,
+        new_block,
+        new_block,
+    )
 
     def onward(value, axis):
         return lax.ppermute(value, axis, [(i, i + 1) for i in range(lax.axis_size(axis) - 1)])
@@ -621,20 +713,24 @@
     def backward(value, axis):
         return lax.ppermute(value, axis, [(i + 1, i) for i in range(lax.axis_size(axis) - 1)])
 
-    y_before = onward(y_top, "gy")
-    x_before = onward(x_top, "gx")
-    y_after = backward(y_low, "gy")
-    x_after = backward(x_low, "gx")
+    y_before = onward(y_top, ALONG_Y)
+    x_before = onward(x_top, ALONG_X)
+    y_after = backward(y_low, ALONG_Y)
+    x_after = backward(x_low, ALONG_X)
 
     stack_rows = 2 * LANES + 4 * ALL + 2 * NEW
     stack_width = GROUP * CHUNKS * LANES
     gram, sensed = pl.pallas_call(
         gram_kernel,
-        grid=(1,),
         out_shape=[shape(stack_rows, 2 * LANES), shape(ALL, LANES)],
-        in_specs=[scalar, whole] + field_specs + columns(NEW * ROWS),
+        in_specs=[scalar, whole] + [hbm] * 3,
         out_specs=[whole] * 2,
-        scratch_shapes=[pltpu.VMEM((stack_rows, stack_width), BF16)] * 2,
+        scratch_shapes=[
+            pltpu.VMEM((stack_rows, stack_width), BF16),
+            pltpu.VMEM((ROWS, ALL, width_yz), F32),
+            pltpu.VMEM((ROWS, NEW, width_yz), F32),
+            pltpu.SemaphoreType.DMA((ROWS,)),
+        ],
         compiler_params=params,
         cost_estimate=pl.CostEstimate(
             flops=2 * stack_rows * 2 * LANES * width_x * width_yz,
@@ -642,12 +738,15 @@
             transcendentals=0,
         ),
         name="gram",
-    )(places, coef, *fields, *([source] * CHUNKS))
+    )(sensor_cells, coef, old_basis, new_block, source_matrix)
+    y_before, y_after, x_before, x_after, gram = lax.optimization_barrier(
+        (y_before, y_after, x_before, x_after, gram)
+    )
 
     face_width = (HALF + CHUNKS) * LANES
     partial = pl.pallas_call(
         face_kernel,
-        out_shape=shape(2 * ALL, LANES),
+        out_shape=shape(PAYLOAD, LANES),
         in_specs=[whole] * 6,
         out_specs=whole,
         scratch_shapes=[
@@ -662,53 +761,61 @@
 
     results = pl.pallas_call(
         functools.partial(basis_kernel, volume),
-        grid=(1,),
         out_shape=[
-            shape(NEW * ROWS, width_yz),
-            shape(NEW * ROWS, width_yz),
-            shape(ALL, NEW),
+            shape(*new_block.shape),
+            shape(*new_block.shape),
+            shape(NEW, ALL),
             shape(NEW, OLD),
-            shape(ALL, NEW),
+            shape(NEW, ALL),
             shape(16, NEW),
             shape(NEW, NEW),
         ],
-        in_specs=[whole] + [scalar] * 5 + [whole] * 5 + field_specs,
+        in_specs=[whole] + [scalar] * 4 + [whole] * 5 + [hbm] * 2,
         out_specs=[hbm, hbm] + [whole] * 5,
         scratch_shapes=[
+            pltpu.VMEM((ROWS, ALL, width_yz), F32),
             pltpu.VMEM((7 * CHUNKS, ROWS, LANES), F32),
             pltpu.VMEM((ROWS + 2, NEW, width_yz), F32),
+            pltpu.VMEM((ROWS, NEW, width_yz), F32),
             pltpu.VMEM((ROWS, NEW, LANES), F32),
             pltpu.VMEM((ROWS, NEW, LANES), F32),
-            pltpu.VMEM((CHUNKS, NEW * ROWS, LANES), F32),
-            pltpu.VMEM((CHUNKS, NEW * ROWS, LANES), F32),
             pltpu.VMEM((PARTS * LANES, width_yz), BF16),
             pltpu.VMEM((PARTS * LANES, width_yz), BF16),
             pltpu.VMEM((3 * NEW, PARTS * LANES), BF16),
-            pltpu.SemaphoreType.DMA((2 * CHUNKS,)),
+            pltpu.SemaphoreType.DMA((ROWS,)),
+            pltpu.SemaphoreType.DMA((ROWS,)),
+            pltpu.SemaphoreType.DMA((ROWS,)),
         ],
         compiler_params=params,
         name="basis",
-    )(region_map, *tables, shifts, summed, y_before, y_after, x_before, x_after, *fields)
+    )(
+        region_map,
+        *tables,
+        summed,
+        y_before,
+        y_after,
+        x_before,
+        x_after,
+        old_basis,
+        new_block,
+    )
+    basis, applied, stiff_block, stiff_row, capacity_block, sensor_block, source_block = results
     return (
-        results[0].reshape(new_block.shape),
-        results[1].reshape(new_block.shape),
-        *results[2:],
+        basis,
+        applied,
+        stiff_block.T,
+        stiff_row,
+        capacity_block.T,
+        sensor_block,
+        source_block,
     )
 
 
 def solution(mesh):
-    in_specs = (
-        P(None, "gx", "gy"),
-        P(None, "gx", "gy"),
-        P(None, "gx", "gy"),
-        P("gx", "gy"),
-        P(),
-        P(),
-        P(),
-        P(),
-        P(),
-    )
-    out_specs = (P(None, "gx", "gy"), P(None, "gx", "gy"), P(), P(), P(), P(), P())
+    mesh = jax.sharding.Mesh(mesh.devices.reshape(4, 2, 8, 4), ALONG_X + ALONG_Y)
+    fields = P(None, ALONG_X, ALONG_Y)
+    in_specs = (fields, fields, fields, P(ALONG_X, ALONG_Y), P(), P(), P(), P(), P())
+    out_specs = (fields, fields, P(), P(), P(), P(), P())
     return jax.shard_map(
         per_device, mesh=mesh, in_specs=in_specs, out_specs=out_specs, check_vma=False
     )

time: 154 us -> 106 us (0.69)
  the two profiles are of different devices: /device:TPU:40 before, /device:TPU:1 now
where the time goes in v2:
time: 106 us
  Pallas kernels  47.9 us (45%)
  blocking collectives  44.6 us (42%)
  starting transfers between devices  11.3 us (11%)
    all_to_all x3, blocking collectives, swap(): return lax.all_to_all(pieces, axes, 0, 0)  44.6 us
    pallas_call x1, Pallas kernels, per_device(): pl.pallas_call(functools.partial(basis_kernel, volume), out_shape=[shape(...  21.1 us
    pallas_call x1, Pallas kernels, per_device(): pl.pallas_call(gram_kernel, out_shape=[shape(stack_rows, 2 * LANES), shap...  18.4 us
    ppermute x2, starting transfers between devices, onward(): lax.ppermute(value, axis, [(i, i + 1) for i in range(lax.axis_size(axis)...  8.04 us
    pallas_call x1, Pallas kernels, per_device(): pl.pallas_call(pack_kernel, grid=(1,), out_shape=[shape(HALF, FACE, LANES...  5.23 us
    ppermute x2, starting transfers between devices, backward(): lax.ppermute(value, axis, [(i + 1, i) for i in range(lax.axis_size(axis)...  3.21 us
    pallas_call x1, Pallas kernels, per_device(): pl.pallas_call(face_kernel, out_shape=shape(PAYLOAD, LANES), in_specs=[wh...  3.17 us
  transfers between devices with their start and end apart: 4, of which 0 were waited for; matrix products, arithmetic and copies ran while one was open for 0% of the time, Pallas kernels for 17%

profile of v2, /device:TPU:1, one launch (start us, length us, event | category | flops | bytes accessed | tf_op | source)
XLA Modules:
  0.0 105.6 jit_solution(7263354463469634771)
XLA Ops:
  0.6 5.2 %pack.1 = (f32[16,104,128]{2,1,0:T(8,128)}, f32[16,104,128]{2,1,0:T(8,128)}, f32[4,112,128]{2,1,0:T(8,128)}, f32[4,112,128]{2,1,0:T(8,128)}, f32[32,32,128]{2,1,0:T(8,128)}) custom-call(s32[32,512]{1,0:T(8,128)} %region_ref.3, f32[8]{0:T(128)} %conductivity.3, f32[8]{0:T(128)} %damping.3, f32[8]{0:T(128)} %drift_speed.3, f32[8]{0:T(128)} %heat_capacity.3, ...), custom_call_target="tpu_custom_call" | custom-call | tf_op jit(solution)/shard_map/pack/pallas_call | solution.py:681
  5.9 4.1 %collective-permute-start = (f32[16,104,128]{2,1,0:T(8,128)}, f32[16,104,128]{2,1,0:T(8,128)S(1)}, u32[]{:S(2)}, u32[]{:S(2)}) collective-permute-start(f32[16,104,128]{2,1,0:T(8,128)} %get-tuple-element.26), channel_id=1, source_target_pairs={{0,1},{1,2},{2,3},{3,4},{4,5},{5,6},{6,7},{7,8},{8,9},{9,10},{10,1... | collective-permute-start | bytes 2555912 | tf_op jit(solution)/shard_map/ppermute | solution.py:711
  10.0 1.3 %collective-permute-start.1 = (f32[16,104,128]{2,1,0:T(8,128)}, f32[16,104,128]{2,1,0:T(8,128)S(1)}, u32[]{:S(2)}, u32[]{:S(2)}) collective-permute-start(f32[16,104,128]{2,1,0:T(8,128)} %get-tuple-element.27.y_own), channel_id=1, source_target_pairs={{1,0},{2,1},{3,2},{4,3},{5,4},{6,5},{7,6},{8,7},{9,8},{10,9},{11,1... | collective-permute-start | bytes 2555912 | tf_op jit(solution)/shard_map/ppermute | solution.py:714
  11.3 4.0 %collective-permute-start.2 = (f32[4,112,128]{2,1,0:T(8,128)}, f32[4,112,128]{2,1,0:T(8,128)S(1)}, u32[]{:S(2)}, u32[]{:S(2)}) collective-permute-start(f32[4,112,128]{2,1,0:T(8,128)} %get-tuple-element.28), channel_id=1, source_target_pairs={{0,32},{32,64},{64,96},{96,128},{128,160},{160,192},{192,224},{1,3... | collective-permute-start | bytes 688136 | tf_op jit(solution)/shard_map/ppermute | solution.py:711
  15.2 1.9 %collective-permute-start.3 = (f32[4,112,128]{2,1,0:T(8,128)}, f32[4,112,128]{2,1,0:T(8,128)S(1)}, u32[]{:S(2)}, u32[]{:S(2)}) collective-permute-start(f32[4,112,128]{2,1,0:T(8,128)} %get-tuple-element.29.x_own), channel_id=1, source_target_pairs={{32,0},{64,32},{96,64},{128,96},{160,128},{192,160},{224,192},{33,... | collective-permute-start | bytes 688136 | tf_op jit(solution)/shard_map/ppermute | solution.py:714
  17.2 18.4 %gram.1 = (f32[704,256]{1,0:T(8,128)}, f32[96,128]{1,0:T(8,128)}) custom-call(s32[16]{0:T(128)} %sensor_cells.1, f32[32,32,128]{2,1,0:T(8,128)} %get-tuple-element.30.coef, f32[64,32,512]{2,1,0:T(8,128)} %old.5, f32[32,32,512]{2,1,0:T(8,128)} %new.5, f32[32,32,512]{2,1,0:T(8,128)} %source.1), custom_call_target="tpu_custom_call" | custom-call | flops 5905580032 | bytes 8388608 | tf_op jit(solution)/shard_map/gram/pallas_call | solution.py:723
  35.6 0.0 collective-permute-done.2.x_near.x_before
  35.6 0.0 copy-start.1
  35.6 0.0 collective-permute-done.3.x_after
  35.6 0.0 copy-start.3
  35.6 0.0 collective-permute-done.y_near.y_before
  35.6 0.0 copy-start
  35.7 0.0 collective-permute-done.1.y_after
  35.7 0.0 copy-start.2
  35.7 0.6 copy-done.1
  36.3 0.3 copy-done
  36.6 3.2 %faces.1 = f32[256,128]{1,0:T(8,128)} custom-call(f32[704,256]{1,0:T(8,128)} %get-tuple-element.32.gram, f32[96,128]{1,0:T(8,128)} %get-tuple-element.33.sensed, f32[16,104,128]{2,1,0:T(8,128)} %get-tuple-element.27.y_own, f32[16,104,128]{2,1,0:T(8,128)} %copy-done, f32[4,112,128]{2,1,0:T(8,128)} %get-tuple-element.29.x_own, f32[4,112,128]{2,1,0:T(8,128)} %copy-done.1), custom_call_target="tpu_custom_call" | custom-call | tf_op jit(solution)/shard_map/faces/pallas_call | solution.py:747
  39.8 20.2 %all_to_all.15 = f32[16,16,128]{2,1,0:T(8,128)S(1)} all-to-all(f32[16,16,128]{2,1,0:T(8,128)} %bitcast.5), channel_id=1, replica_groups=mesh['x'=4,'core'=2,'z'=8,'y'=4] {'core','z'}, dimensions={0} | all-to-all | bytes 262144 | tf_op jit(solution)/shard_map/all_to_all | solution.py:629
  60.0 11.3 %all_to_all.16 = f32[16,16,128]{2,1,0:T(8,128)S(1)} all-to-all(f32[16,16,128]{2,1,0:T(8,128)S(1)} %broadcast_in_dim.4), channel_id=1, replica_groups=mesh['x'=4,'core'=2,'z'=8,'y'=4] {'x','y'}, dimensions={0} | all-to-all | bytes 262144 | tf_op jit(solution)/shard_map/all_to_all | solution.py:629
  71.4 13.1 %all_to_all.17 = f32[16,16,128]{2,1,0:T(8,128)} all-to-all(f32[16,16,128]{2,1,0:T(8,128)S(1)} %broadcast_in_dim.5), channel_id=1, replica_groups=mesh['x'=4,'core'=2,'z'=8,'y'=4] {'core','z'}, dimensions={0} | all-to-all | bytes 262144 | tf_op jit(solution)/shard_map/all_to_all | solution.py:629
  84.5 0.0 copy-done.2
  84.5 0.0 copy-done.3
  84.5 21.1 %basis.1 = (f32[32,32,512]{2,1,0:T(8,128)}, f32[32,32,512]{2,1,0:T(8,128)}, f32[32,96]{1,0:T(8,128)}, f32[32,64]{1,0:T(8,128)}, f32[32,96]{1,0:T(8,128)}, /*index=5*/f32[16,32]{1,0:T(8,128)}, f32[32,32]{1,0:T(8,128)}) custom-call(s32[32,512]{1,0:T(8,128)} %region_ref.3, f32[8]{0:T(128)} %conductivity.3, f32[8]{0:T(128)} %damping.3, f32[8]{0:T(128)} %drift_speed.3, ...), custom_call_target="tpu_custom_call" | custom-call | tf_op jit(solution)/shard_map/basis/pallas_call | solution.py:762
  (4 shorter events, 0.1 us)
Async XLA Ops:
  5.9 29.8 %collective-permute-start = (f32[16,104,128]{2,1,0:T(8,128)}, f32[16,104,128]{2,1,0:T(8,128)S(1)}, u32[]{:S(2)}, u32[]{:S(2)}) collective-permute-start(f32[16,104,128]{2,1,0:T(8,128)} %get-tuple-element.26), channel_id=1, source_target_pairs={{0,1},{1,2},{2,3},{3,4},{4,5},{5,6},{6,7},{7,8},{8,9},{9,10},{10,1... | collective-permute-start | bytes 2555912 | tf_op jit(solution)/shard_map/ppermute | solution.py:711
  10.0 25.7 %collective-permute-start.1 = (f32[16,104,128]{2,1,0:T(8,128)}, f32[16,104,128]{2,1,0:T(8,128)S(1)}, u32[]{:S(2)}, u32[]{:S(2)}) collective-permute-start(f32[16,104,128]{2,1,0:T(8,128)} %get-tuple-element.27.y_own), channel_id=1, source_target_pairs={{1,0},{2,1},{3,2},{4,3},{5,4},{6,5},{7,6},{8,7},{9,8},{10,9},{11,1... | collective-permute-start | bytes 2555912 | tf_op jit(solution)/shard_map/ppermute | solution.py:714
  11.3 24.3 %collective-permute-start.2 = (f32[4,112,128]{2,1,0:T(8,128)}, f32[4,112,128]{2,1,0:T(8,128)S(1)}, u32[]{:S(2)}, u32[]{:S(2)}) collective-permute-start(f32[4,112,128]{2,1,0:T(8,128)} %get-tuple-element.28), channel_id=1, source_target_pairs={{0,32},{32,64},{64,96},{96,128},{128,160},{160,192},{192,224},{1,3... | collective-permute-start | bytes 688136 | tf_op jit(solution)/shard_map/ppermute | solution.py:711
  15.2 20.4 %collective-permute-start.3 = (f32[4,112,128]{2,1,0:T(8,128)}, f32[4,112,128]{2,1,0:T(8,128)S(1)}, u32[]{:S(2)}, u32[]{:S(2)}) collective-permute-start(f32[4,112,128]{2,1,0:T(8,128)} %get-tuple-element.29.x_own), channel_id=1, source_target_pairs={{32,0},{64,32},{96,64},{128,96},{160,128},{192,160},{224,192},{33,... | collective-permute-start | bytes 688136 | tf_op jit(solution)/shard_map/ppermute | solution.py:714
  35.6 0.7 copy-start.1
  35.6 48.9 %copy-start.3 = (f32[4,112,128]{2,1,0:T(8,128)}, f32[4,112,128]{2,1,0:T(8,128)S(1)}, u32[]{:S(2)}) copy-start(f32[4,112,128]{2,1,0:T(8,128)S(1)} %collective-permute-done.3.x_after) | copy-start | bytes 688132
  35.6 1.0 copy-start
  35.7 48.8 %copy-start.2 = (f32[16,104,128]{2,1,0:T(8,128)}, f32[16,104,128]{2,1,0:T(8,128)S(1)}, u32[]{:S(2)}) copy-start(f32[16,104,128]{2,1,0:T(8,128)S(1)} %collective-permute-done.1.y_after) | copy-start | bytes 2555908

commit v3 on v2

--- a/solution.py
+++ b/solution.py
@@ -65,11 +65,22 @@
     return stiff, table_mean(heat_capacity)
 
 
-def row_copies(old, new, rows, sems, x):
-    return [
-        pltpu.make_async_copy(old.at[:, x, :], rows.at[x, pl.ds(0, OLD), :], sems.at[x]),
-        pltpu.make_async_copy(new.at[:, x, :], rows.at[x, pl.ds(OLD, NEW), :], sems.at[x]),
-    ]
+def turn(source, target, start, shift, fields, base):
+    for f in range(0, fields, 8):
+        for j in range(CHUNKS):
+            here = slice(j * LANES, (j + 1) * LANES)
+            tile = source[f : f + 8, pl.ds(start, 8), here]
+            target[pl.ds(start + shift, 8), base + f : base + f + 8, here] = jnp.transpose(
+                tile, (1, 0, 2)
+            )
+
+
+def turn_back(source, target, start, shift, fields):
+    for f in range(0, fields, 8):
+        for j in range(CHUNKS):
+            here = slice(j * LANES, (j + 1) * LANES)
+            tile = source[pl.ds(start + shift, 8), f : f + 8, here]
+            target[f : f + 8, pl.ds(start, 8), here] = jnp.transpose(tile, (1, 0, 2))
 
 
 def cell_fields(region_ref, conductivity, damping, drift_speed, heat_capacity):
@@ -205,37 +216,33 @@
         copy.wait()
 
 
-def gram_kernel(sensor_cells, coef, old, new, source, out, sensed, stack, rows, sources, sems):
+def gram_kernel(
+    sensor_cells, coef, old, new, source, out, sensed, rows_out, first, second, old_raw, new_raw, source_raw, rows, sources, sems, out_sems
+):
     width = CHUNKS * LANES
-
-    def incoming(x):
-        return row_copies(old, new, rows, sems, x) + [
-            pltpu.make_async_copy(source.at[:, x, :], sources.at[x], sems.at[x])
+    groups = ROWS // GROUP
+    low_half = lanes_of((1, LANES)) < NZ
+
+    def incoming(block):
+        at = pl.ds(pl.multiple_of(block * 8, 8), 8)
+        return [
+            pltpu.make_async_copy(field.at[:, at, :], raw.at[:, at, :], sems.at[k, block])
+            for k, (field, raw) in enumerate(
+                ((old, old_raw), (new, new_raw), (source, source_raw))
+            )
         ]
 
-    def begin(x, carry):
-        for copy in incoming(x):
-            copy.start()
-        return carry
-
-    lax.fori_loop(0, ROWS, begin, 0)
-    low_half = lanes_of((1, LANES)) < NZ
-    zero_rows = jnp.zeros((LANES - ALL, stack.shape[1]), BF16)
-    stack[ALL:LANES, :] = zero_rows
-    stack[LANES + ALL : 2 * LANES, :] = zero_rows
-    out[...] = jnp.zeros(out.shape, F32)
-
-    def arrive(x):
-        for copy in incoming(x):
+    def arrange(block):
+        for copy in incoming(block):
             copy.wait()
-
-    def fill(group):
+        start = pl.multiple_of(block * 8, 8)
+        turn(old_raw, rows, start, 0, OLD, 0)
+        turn(new_raw, rows, start, 0, NEW, OLD)
+        turn(source_raw, sources, start, 0, NEW, 0)
+
+    def fill(stack, group):
         for r in range(GROUP):
             x = group * GROUP + r
-            if r < GROUP - 1:
-                arrive(x + 1)
-            else:
-                pl.when(x + 1 < ROWS)(lambda: arrive(x + 1))
             below = jnp.maximum(x - 1, 0)
             above = jnp.minimum(x + 1, ROWS - 1)
             mid = [rows[x, :, j * LANES : (j + 1) * LANES] for j in range(CHUNKS)]
@@ -262,29 +269,49 @@
                 high, low = split(value, 2)
                 stack[0:ALL, at] = high
                 stack[LANES : LANES + ALL, at] = low
+                high, low = split(sources[x, :, here], 2)
+                stack[ALL:LANES, at] = high
+                stack[LANES + ALL : 2 * LANES, at] = low
                 base = 2 * LANES
                 for item in (moved, scale(7) * value):
                     high, low = split(item, 2)
                     stack[base : base + ALL, at] = high
                     stack[base + ALL : base + 2 * ALL, at] = low
                     base += 2 * ALL
-                high, low = split(sources[x, :, here], 2)
-                stack[base : base + NEW, at] = high
-                stack[base + NEW : base + 2 * NEW, at] = low
-
-    arrive(0)
-
-    def step(i, carry):
-        fill(i)
+
+    def add(stack):
         out[...] += lax.dot_general(
             stack[...],
             stack[0 : 2 * LANES, :],
             (((1,), (1,)), ((), ())),
             preferred_element_type=F32,
         )
+
+    for block in range(ROWS // 8):
+        for copy in incoming(block):
+            copy.start()
+    out[...] = jnp.zeros(out.shape, F32)
+    arrange(0)
+    fill(first, 0)
+
+    def step(i, carry):
+        arrange(i + 1)
+        add(first)
+        fill(second, 2 * i + 1)
+        add(second)
+        fill(first, 2 * i + 2)
         return carry
 
-    lax.fori_loop(0, ROWS // GROUP, step, 0)
+    lax.fori_loop(0, groups // 2 - 1, step, 0)
+    outgoing = [
+        pltpu.make_async_copy(rows.at[pl.ds(x, 8)], rows_out.at[pl.ds(x, 8)], out_sems.at[x // 8])
+        for x in range(0, ROWS, 8)
+    ]
+    for copy in outgoing:
+        copy.start()
+    add(first)
+    fill(second, groups - 1)
+    add(second)
 
     lane = lanes_of((ALL, LANES))
     sensed[...] = jnp.zeros(sensed.shape, F32)
@@ -311,6 +338,8 @@
         return carry
 
     lax.fori_loop(0, sensor_cells.shape[0], sense, 0)
+    for copy in outgoing:
+        copy.wait()
 
 
 def fold(block, rows):
@@ -347,17 +376,13 @@
     faces = lax.dot_general(
         diffs[...], scaled[...], (((1,), (1,)), ((), ())), preferred_element_type=F32
     )
+    crossed = fold(gram[0 : 2 * LANES, :], LANES)
+    overlap = crossed[0:ALL]
+    source = crossed[ALL:LANES]
     base = 2 * LANES
-    overlap = (
-        gram[0:ALL, 0:LANES]
-        + gram[0:ALL, LANES:]
-        + (gram[LANES : LANES + ALL, 0:LANES] + gram[LANES : LANES + ALL, LANES:])
-    )
     moved = fold(gram[base : base + 2 * ALL, :], ALL) - fold(faces, ALL)
     base += 2 * ALL
     massed = fold(gram[base : base + 2 * ALL, :], ALL)
-    base += 2 * ALL
-    source = fold(gram[base : base + 2 * NEW, :], NEW)
     source = jnp.concatenate([source, jnp.zeros((LANES - NEW, LANES), F32)], axis=0).T
     source = pltpu.roll(source[0:ALL, :], ALL, 1)
     lane = lanes_of((ALL, LANES))
@@ -412,8 +437,7 @@
     y_after,
     x_before,
     x_after,
-    old,
-    new,
+    rows_in,
     basis_out,
     applied_out,
     stiff_block,
@@ -425,6 +449,8 @@
     coef,
     field,
     applied,
+    basis_raw,
+    applied_raw,
     low_y,
     high_y,
     first,
@@ -436,12 +462,12 @@
 ):
     width = CHUNKS * LANES
 
-    def begin(x, carry):
-        for copy in row_copies(old, new, rows, sems, x):
-            copy.start()
-        return carry
-
-    lax.fori_loop(0, ROWS, begin, 0)
+    incoming = [
+        pltpu.make_async_copy(rows_in.at[pl.ds(x, 8)], rows.at[pl.ds(x, 8)], sems.at[x // 8])
+        for x in range(0, ROWS, 8)
+    ]
+    for copy in incoming:
+        copy.start()
     shifts = common_shifts(conductivity, damping, drift_speed, heat_capacity)
 
     lane = lanes_of((ALL, LANES))
@@ -543,19 +569,26 @@
                 target[r + HALF] = turned if at_low else tile
 
     def load(stack, x):
-        for copy in row_copies(old, new, rows, sems, x):
-            copy.wait()
         fill(stack, [rows[x, :, j * LANES : (j + 1) * LANES] for j in range(CHUNKS)])
 
-    def basis_copy(x):
-        return pltpu.make_async_copy(field.at[x + 1], basis_out.at[:, x, :], basis_sems.at[x])
-
-    def applied_copy(x):
-        return pltpu.make_async_copy(applied.at[x], applied_out.at[:, x, :], applied_sems.at[x])
+    def outgoing(block):
+        at = pl.ds(pl.multiple_of(block * 8, 8), 8)
+        return [
+            pltpu.make_async_copy(basis_raw.at[:, at, :], basis_out.at[:, at, :], basis_sems.at[block]),
+            pltpu.make_async_copy(
+                applied_raw.at[:, at, :], applied_out.at[:, at, :], applied_sems.at[block]
+            ),
+        ]
+
+    def flush(block):
+        start = pl.multiple_of(block * 8, 8)
+        turn_back(field, basis_raw, start, 1, NEW)
+        turn_back(applied, applied_raw, start, 0, NEW)
+        for copy in outgoing(block):
+            copy.start()
 
     def keep(x, stack):
         field[x + 1] = product(stack)
-        basis_copy(x).start()
 
     def apply(x):
         mid = [field[x + 1, :, j * LANES : (j + 1) * LANES] for j in range(CHUNKS)]
@@ -580,8 +613,9 @@
                 + scale(5) * pltpu.roll(value, LANES - 1, 1)
                 + scale(6) * value
             )
-        applied_copy(x).start()
-
+
+    for copy in incoming:
+        copy.wait()
     load(first, 0)
     load(second, 1)
     keep(0, first)
@@ -594,12 +628,14 @@
         keep(x + 1, first)
         load(second, x + 2)
         apply(x)
+        pl.when((i + 1) % 4 == 0)(lambda: flush((i + 1) // 4 - 1))
         return carry
 
     lax.fori_loop(0, ROWS // 2 - 1, step, 0)
     keep(ROWS - 1, second)
     apply(ROWS - 2)
     apply(ROWS - 1)
+    flush(ROWS // 8 - 1)
 
     outside = small_dot(left_over, flip(inverse))
     unit = jnp.where(
@@ -617,12 +653,9 @@
     sensor_block[...] = flip(small_dot(mix, sensed))
     source_block[...] = small_dot(mix, source)
 
-    def finish(x, carry):
-        basis_copy(x).wait()
-        applied_copy(x).wait()
-        return carry
-
-    lax.fori_loop(0, ROWS, finish, 0)
+    for block in range(ROWS // 8):
+        for copy in outgoing(block):
+            copy.wait()
 
 
 def swap(pieces, axes):
@@ -718,18 +751,27 @@
     y_after = backward(y_low, ALONG_Y)
     x_after = backward(x_low, ALONG_X)
 
-    stack_rows = 2 * LANES + 4 * ALL + 2 * NEW
+    stack_rows = 2 * LANES + 4 * ALL
     stack_width = GROUP * CHUNKS * LANES
-    gram, sensed = pl.pallas_call(
+    gram, sensed, rows = pl.pallas_call(
         gram_kernel,
-        out_shape=[shape(stack_rows, 2 * LANES), shape(ALL, LANES)],
+        out_shape=[
+            shape(stack_rows, 2 * LANES),
+            shape(ALL, LANES),
+            shape(ROWS, ALL, width_yz),
+        ],
         in_specs=[scalar, whole] + [hbm] * 3,
-        out_specs=[whole] * 2,
+        out_specs=[whole, whole, hbm],
         scratch_shapes=[
             pltpu.VMEM((stack_rows, stack_width), BF16),
+            pltpu.VMEM((stack_rows, stack_width), BF16),
+            pltpu.VMEM(old_basis.shape, F32),
+            pltpu.VMEM(new_block.shape, F32),
+            pltpu.VMEM(source_matrix.shape, F32),
             pltpu.VMEM((ROWS, ALL, width_yz), F32),
             pltpu.VMEM((ROWS, NEW, width_yz), F32),
-            pltpu.SemaphoreType.DMA((ROWS,)),
+            pltpu.SemaphoreType.DMA((3, 4)),
+            pltpu.SemaphoreType.DMA((4,)),
         ],
         compiler_params=params,
         cost_estimate=pl.CostEstimate(
@@ -770,21 +812,23 @@
             shape(16, NEW),
             shape(NEW, NEW),
         ],
-        in_specs=[whole] + [scalar] * 4 + [whole] * 5 + [hbm] * 2,
+        in_specs=[whole] + [scalar] * 4 + [whole] * 5 + [hbm],
         out_specs=[hbm, hbm] + [whole] * 5,
         scratch_shapes=[
             pltpu.VMEM((ROWS, ALL, width_yz), F32),
             pltpu.VMEM((7 * CHUNKS, ROWS, LANES), F32),
             pltpu.VMEM((ROWS + 2, NEW, width_yz), F32),
             pltpu.VMEM((ROWS, NEW, width_yz), F32),
+            pltpu.VMEM(new_block.shape, F32),
+            pltpu.VMEM(new_block.shape, F32),
             pltpu.VMEM((ROWS, NEW, LANES), F32),
             pltpu.VMEM((ROWS, NEW, LANES), F32),
             pltpu.VMEM((PARTS * LANES, width_yz), BF16),
             pltpu.VMEM((PARTS * LANES, width_yz), BF16),
             pltpu.VMEM((3 * NEW, PARTS * LANES), BF16),
-            pltpu.SemaphoreType.DMA((ROWS,)),
-            pltpu.SemaphoreType.DMA((ROWS,)),
-            pltpu.SemaphoreType.DMA((ROWS,)),
+            pltpu.SemaphoreType.DMA((4,)),
+            pltpu.SemaphoreType.DMA((4,)),
+            pltpu.SemaphoreType.DMA((4,)),
         ],
         compiler_params=params,
         name="basis",
@@ -796,8 +840,7 @@
         y_after,
         x_before,
         x_after,
-        old_basis,
-        new_block,
+        rows,
     )
     basis, applied, stiff_block, stiff_row, capacity_block, sensor_block, source_block = results
     return (

time: 106 us -> 102 us (0.962)
  Pallas kernels: 47.9 us -> 43.8 us
    pallas_call x1, Pallas kernels: 21.1 us -> 17.9 us  [per_device(): pl.pallas_call(functools.partial(basis_kernel, volume), out_shape=[shape(...]
where the time goes in v3:
time: 102 us
  blocking collectives  44.6 us (44%)
  Pallas kernels  43.8 us (43%)
  starting transfers between devices  11.3 us (11%)
    all_to_all x3, blocking collectives, swap(): return lax.all_to_all(pieces, axes, 0, 0)  44.6 us
    pallas_call x1, Pallas kernels, per_device(): pl.pallas_call(functools.partial(basis_kernel, volume), out_shape=[shape(...  17.9 us
    pallas_call x1, Pallas kernels, per_device(): pl.pallas_call(gram_kernel, out_shape=[shape(stack_rows, 2 * LANES), shap...  17.4 us
    ppermute x2, starting transfers between devices, onward(): lax.ppermute(value, axis, [(i, i + 1) for i in range(lax.axis_size(axis)...  8.04 us
    pallas_call x1, Pallas kernels, per_device(): pl.pallas_call(pack_kernel, grid=(1,), out_shape=[shape(HALF, FACE, LANES...  5.25 us
    ppermute x2, starting transfers between devices, backward(): lax.ppermute(value, axis, [(i + 1, i) for i in range(lax.axis_size(axis)...  3.21 us
    pallas_call x1, Pallas kernels, per_device(): pl.pallas_call(face_kernel, out_shape=shape(PAYLOAD, LANES), in_specs=[wh...  3.15 us
  transfers between devices with their start and end apart: 4, of which 0 were waited for; matrix products, arithmetic and copies ran while one was open for 0% of the time, Pallas kernels for 17%

profile of v3, /device:TPU:1, one launch (start us, length us, event | category | flops | bytes accessed | tf_op | source)
XLA Modules:
  0.0 101.6 jit_solution(13715066680357773589)
XLA Ops:
  0.6 5.2 %pack.1 = (f32[16,104,128]{2,1,0:T(8,128)}, f32[16,104,128]{2,1,0:T(8,128)}, f32[4,112,128]{2,1,0:T(8,128)}, f32[4,112,128]{2,1,0:T(8,128)}, f32[32,32,128]{2,1,0:T(8,128)}) custom-call(s32[32,512]{1,0:T(8,128)} %region_ref.3, f32[8]{0:T(128)} %conductivity.3, f32[8]{0:T(128)} %damping.3, f32[8]{0:T(128)} %drift_speed.3, f32[8]{0:T(128)} %heat_capacity.3, ...), custom_call_target="tpu_custom_call" | custom-call | tf_op jit(solution)/shard_map/pack/pallas_call | solution.py:714
  5.9 4.1 %collective-permute-start = (f32[16,104,128]{2,1,0:T(8,128)}, f32[16,104,128]{2,1,0:T(8,128)S(1)}, u32[]{:S(2)}, u32[]{:S(2)}) collective-permute-start(f32[16,104,128]{2,1,0:T(8,128)} %get-tuple-element.27), channel_id=1, source_target_pairs={{0,1},{1,2},{2,3},{3,4},{4,5},{5,6},{6,7},{7,8},{8,9},{9,10},{10,1... | collective-permute-start | bytes 2555912 | tf_op jit(solution)/shard_map/ppermute | solution.py:744
  10.0 1.3 %collective-permute-start.1 = (f32[16,104,128]{2,1,0:T(8,128)}, f32[16,104,128]{2,1,0:T(8,128)S(1)}, u32[]{:S(2)}, u32[]{:S(2)}) collective-permute-start(f32[16,104,128]{2,1,0:T(8,128)} %get-tuple-element.28.y_own), channel_id=1, source_target_pairs={{1,0},{2,1},{3,2},{4,3},{5,4},{6,5},{7,6},{8,7},{9,8},{10,9},{11,1... | collective-permute-start | bytes 2555912 | tf_op jit(solution)/shard_map/ppermute | solution.py:747
  11.3 4.0 %collective-permute-start.2 = (f32[4,112,128]{2,1,0:T(8,128)}, f32[4,112,128]{2,1,0:T(8,128)S(1)}, u32[]{:S(2)}, u32[]{:S(2)}) collective-permute-start(f32[4,112,128]{2,1,0:T(8,128)} %get-tuple-element.29), channel_id=1, source_target_pairs={{0,32},{32,64},{64,96},{96,128},{128,160},{160,192},{192,224},{1,3... | collective-permute-start | bytes 688136 | tf_op jit(solution)/shard_map/ppermute | solution.py:744
  15.2 1.9 %collective-permute-start.3 = (f32[4,112,128]{2,1,0:T(8,128)}, f32[4,112,128]{2,1,0:T(8,128)S(1)}, u32[]{:S(2)}, u32[]{:S(2)}) collective-permute-start(f32[4,112,128]{2,1,0:T(8,128)} %get-tuple-element.30.x_own), channel_id=1, source_target_pairs={{32,0},{64,32},{96,64},{128,96},{160,128},{192,160},{224,192},{33,... | collective-permute-start | bytes 688136 | tf_op jit(solution)/shard_map/ppermute | solution.py:747
  17.2 17.4 %gram.1 = (f32[640,256]{1,0:T(8,128)}, f32[96,128]{1,0:T(8,128)}, f32[32,96,512]{2,1,0:T(8,128)}) custom-call(s32[16]{0:T(128)} %sensor_cells.1, f32[32,32,128]{2,1,0:T(8,128)} %get-tuple-element.31.coef, f32[64,32,512]{2,1,0:T(8,128)} %old.3, f32[32,32,512]{2,1,0:T(8,128)} %new.3, f32[32,32,512]{2,1,0:T(8,128)} %source.1), custom_call_target="tpu_custom_call" | custom-call | flops 5368709120 | bytes 8388608 | tf_op jit(solution)/shard_map/gram/pallas_call | solution.py:756
  34.6 0.0 collective-permute-done.2.x_near.x_before
  34.6 0.0 copy-start.1
  34.6 0.0 collective-permute-done.3.x_after
  34.7 0.0 copy-start.3
  34.7 0.0 collective-permute-done.y_near.y_before
  34.7 0.0 copy-start
  34.7 0.0 collective-permute-done.1.y_after
  34.7 0.0 copy-start.2
  34.7 0.6 copy-done.1
  35.3 0.3 copy-done
  35.6 3.1 %faces.1 = f32[256,128]{1,0:T(8,128)} custom-call(f32[640,256]{1,0:T(8,128)} %get-tuple-element.33.gram, f32[96,128]{1,0:T(8,128)} %get-tuple-element.34.sensed, f32[16,104,128]{2,1,0:T(8,128)} %get-tuple-element.28.y_own, f32[16,104,128]{2,1,0:T(8,128)} %copy-done, f32[4,112,128]{2,1,0:T(8,128)} %get-tuple-element.30.x_own, f32[4,112,128]{2,1,0:T(8,128)} %copy-done.1), custom_call_target="tpu_custom_call" | custom-call | tf_op jit(solution)/shard_map/faces/pallas_call | solution.py:789
  38.8 20.2 %all_to_all.15 = f32[16,16,128]{2,1,0:T(8,128)S(1)} all-to-all(f32[16,16,128]{2,1,0:T(8,128)} %bitcast.5), channel_id=1, replica_groups=mesh['x'=4,'core'=2,'z'=8,'y'=4] {'core','z'}, dimensions={0} | all-to-all | bytes 262144 | tf_op jit(solution)/shard_map/all_to_all | solution.py:662
  59.0 11.1 %all_to_all.16 = f32[16,16,128]{2,1,0:T(8,128)S(1)} all-to-all(f32[16,16,128]{2,1,0:T(8,128)S(1)} %broadcast_in_dim.4), channel_id=1, replica_groups=mesh['x'=4,'core'=2,'z'=8,'y'=4] {'x','y'}, dimensions={0} | all-to-all | bytes 262144 | tf_op jit(solution)/shard_map/all_to_all | solution.py:662
  70.2 13.2 %all_to_all.17 = f32[16,16,128]{2,1,0:T(8,128)} all-to-all(f32[16,16,128]{2,1,0:T(8,128)S(1)} %broadcast_in_dim.5), channel_id=1, replica_groups=mesh['x'=4,'core'=2,'z'=8,'y'=4] {'core','z'}, dimensions={0} | all-to-all | bytes 262144 | tf_op jit(solution)/shard_map/all_to_all | solution.py:662
  83.5 0.0 copy-done.2
  83.5 0.0 copy-done.3
  83.5 17.9 %basis.1 = (f32[32,32,512]{2,1,0:T(8,128)}, f32[32,32,512]{2,1,0:T(8,128)}, f32[32,96]{1,0:T(8,128)}, f32[32,64]{1,0:T(8,128)}, f32[32,96]{1,0:T(8,128)}, /*index=5*/f32[16,32]{1,0:T(8,128)}, f32[32,32]{1,0:T(8,128)}) custom-call(s32[32,512]{1,0:T(8,128)} %region_ref.3, f32[8]{0:T(128)} %conductivity.3, f32[8]{0:T(128)} %damping.3, f32[8]{0:T(128)} %drift_speed.3, ...), custom_call_target="tpu_custom_call" | custom-call | tf_op jit(solution)/shard_map/basis/pallas_call | solution.py:804
  (4 shorter events, 0.1 us)
Async XLA Ops:
  5.9 28.8 %collective-permute-start = (f32[16,104,128]{2,1,0:T(8,128)}, f32[16,104,128]{2,1,0:T(8,128)S(1)}, u32[]{:S(2)}, u32[]{:S(2)}) collective-permute-start(f32[16,104,128]{2,1,0:T(8,128)} %get-tuple-element.27), channel_id=1, source_target_pairs={{0,1},{1,2},{2,3},{3,4},{4,5},{5,6},{6,7},{7,8},{8,9},{9,10},{10,1... | collective-permute-start | bytes 2555912 | tf_op jit(solution)/shard_map/ppermute | solution.py:744
  10.0 24.7 %collective-permute-start.1 = (f32[16,104,128]{2,1,0:T(8,128)}, f32[16,104,128]{2,1,0:T(8,128)S(1)}, u32[]{:S(2)}, u32[]{:S(2)}) collective-permute-start(f32[16,104,128]{2,1,0:T(8,128)} %get-tuple-element.28.y_own), channel_id=1, source_target_pairs={{1,0},{2,1},{3,2},{4,3},{5,4},{6,5},{7,6},{8,7},{9,8},{10,9},{11,1... | collective-permute-start | bytes 2555912 | tf_op jit(solution)/shard_map/ppermute | solution.py:747
  11.3 23.3 %collective-permute-start.2 = (f32[4,112,128]{2,1,0:T(8,128)}, f32[4,112,128]{2,1,0:T(8,128)S(1)}, u32[]{:S(2)}, u32[]{:S(2)}) collective-permute-start(f32[4,112,128]{2,1,0:T(8,128)} %get-tuple-element.29), channel_id=1, source_target_pairs={{0,32},{32,64},{64,96},{96,128},{128,160},{160,192},{192,224},{1,3... | collective-permute-start | bytes 688136 | tf_op jit(solution)/shard_map/ppermute | solution.py:744
  15.2 19.4 %collective-permute-start.3 = (f32[4,112,128]{2,1,0:T(8,128)}, f32[4,112,128]{2,1,0:T(8,128)S(1)}, u32[]{:S(2)}, u32[]{:S(2)}) collective-permute-start(f32[4,112,128]{2,1,0:T(8,128)} %get-tuple-element.30.x_own), channel_id=1, source_target_pairs={{32,0},{64,32},{96,64},{128,96},{160,128},{192,160},{224,192},{33,... | collective-permute-start | bytes 688136 | tf_op jit(solution)/shard_map/ppermute | solution.py:747
  34.6 0.7 copy-start.1
  34.7 48.8 %copy-start.3 = (f32[4,112,128]{2,1,0:T(8,128)}, f32[4,112,128]{2,1,0:T(8,128)S(1)}, u32[]{:S(2)}) copy-start(f32[4,112,128]{2,1,0:T(8,128)S(1)} %collective-permute-done.3.x_after) | copy-start | bytes 688132
  34.7 1.0 copy-start
  34.7 48.8 %copy-start.2 = (f32[16,104,128]{2,1,0:T(8,128)}, f32[16,104,128]{2,1,0:T(8,128)S(1)}, u32[]{:S(2)}) copy-start(f32[16,104,128]{2,1,0:T(8,128)S(1)} %collective-permute-done.1.y_after) | copy-start | bytes 2555908

commit v4 on v3

--- a/solution.py
+++ b/solution.py
@@ -33,6 +33,10 @@
     return lax.axis_index(slow) * lax.axis_size(fast) + lax.axis_index(fast)
 
 
+def odd_lanes(axes):
+    return jnp.broadcast_to(position(axes) % 2, (1, LANES)) == 1
+
+
 def split(value, count):
     pieces = []
     for _ in range(count):
@@ -124,16 +128,21 @@
     old_last,
     new_first,
     new_last,
-    y_top,
-    y_low,
-    x_top,
-    x_low,
+    y_first,
+    y_second,
+    x_first,
+    x_second,
     coef,
     sems,
 ):
     width = CHUNKS * LANES
     copies = []
-    for out, row, base in ((x_top, ROWS - 1, 0), (x_low, 0, 2 * CHUNKS)):
+    odd_x, odd_y = odd_lanes(ALONG_X), odd_lanes(ALONG_Y)
+    parity = position(ALONG_X) % 2
+    for out, row, base in (
+        (x_first, (1 - parity) * (ROWS - 1), 0),
+        (x_second, parity * (ROWS - 1), 2 * CHUNKS),
+    ):
         for j in range(CHUNKS):
             here = pl.ds(j * LANES, LANES)
             for field, start, count, shift in ((old, 0, OLD, 0), (new, OLD, NEW, CHUNKS)):
@@ -165,21 +174,27 @@
             for x in range(0, HALF, 8):
                 at = (slice(x, x + 8), slice(start + f, start + f + 8), slice(None))
                 near, far = turned(last, f, x), turned(last, f, x + HALF)
-                y_top[at] = jnp.where(low_half[None], pltpu.roll(near, NZ, 2), far)
+                top = jnp.where(low_half[None], pltpu.roll(near, NZ, 2), far)
                 near, far = turned(first, f, x), turned(first, f, x + HALF)
-                y_low[at] = jnp.where(low_half[None], near, pltpu.roll(far, NZ, 2))
+                low = jnp.where(low_half[None], near, pltpu.roll(far, NZ, 2))
+                y_first[at] = jnp.where(odd_y[None], low, top)
+                y_second[at] = jnp.where(odd_y[None], top, low)
     near, far = conduct[:HALF, width - LANES :], conduct[HALF:, width - LANES :]
     top_line = jnp.where(low_half, pltpu.roll(near, NZ, 1), far)
     near, far = conduct[:HALF, :LANES], conduct[HALF:, :LANES]
     low_line = jnp.where(low_half, near, pltpu.roll(far, NZ, 1))
+    first_line = jnp.where(odd_y, low_line, top_line)
+    second_line = jnp.where(odd_y, top_line, low_line)
     for r in range(HALF):
-        y_top[r, ALL:FACE, :] = tail(8, top_line[r : r + 1])
-        y_low[r, ALL:FACE, :] = tail(8, low_line[r : r + 1])
+        y_first[r, ALL:FACE, :] = tail(8, first_line[r : r + 1])
+        y_second[r, ALL:FACE, :] = tail(8, second_line[r : r + 1])
     for j in range(CHUNKS):
         here = slice(j * LANES, (j + 1) * LANES)
-        for out, row in ((x_top, ROWS - 1), (x_low, 0)):
-            out[j, ALL : ALL + 8, :] = tail(8, conduct[row : row + 1, here])
-            out[j, ALL + 8 : XFACE, :] = tail(8, drift[row : row + 1, here])
+        for k, value in enumerate((conduct, drift)):
+            at = slice(ALL + 8 * k, ALL + 8 * k + 8)
+            top, low = value[ROWS - 1 : ROWS, here], value[0:1, here]
+            x_first[j, at, :] = tail(8, jnp.where(odd_x, low, top))
+            x_second[j, at, :] = tail(8, jnp.where(odd_x, top, low))
 
     shape = (ROWS, width)
     lane = lanes_of(shape)
@@ -350,7 +365,22 @@
     )
 
 
-def face_kernel(gram, sensed, y_own, y_near, x_own, x_near, out, diffs, scaled):
+def face_kernel(
+    gram,
+    sensed,
+    y_first,
+    y_second,
+    x_first,
+    x_second,
+    y_from_first,
+    y_from_second,
+    x_from_first,
+    x_from_second,
+    out,
+    diffs,
+    scaled,
+):
+    odd_x, odd_y = odd_lanes(ALONG_X), odd_lanes(ALONG_Y)
     tiles = HALF + CHUNKS
     zero_rows = jnp.zeros((LANES - ALL, tiles * LANES), BF16)
     scaled[ALL:LANES, :] = zero_rows
@@ -358,9 +388,11 @@
     for t in range(tiles):
         at = pl.ds(t * LANES, LANES)
         if t < HALF:
-            own, near = y_own.at[t], y_near.at[t]
+            own = jnp.where(odd_y, y_first[t], y_second[t])
+            near = jnp.where(odd_y, y_from_first[t], y_from_second[t])
         else:
-            own, near = x_own.at[t - HALF], x_near.at[t - HALF]
+            own = jnp.where(odd_x, x_first[t - HALF], x_second[t - HALF])
+            near = jnp.where(odd_x, x_from_first[t - HALF], x_from_second[t - HALF])
         value = own[0:ALL, :]
         diff = value - near[0:ALL, :]
         edge = 0.5 * (own[ALL : ALL + 1, :] + near[ALL : ALL + 1, :])
@@ -433,10 +465,10 @@
     drift_speed,
     heat_capacity,
     summed,
-    y_before,
-    y_after,
-    x_before,
-    x_after,
+    y_from_first,
+    y_from_second,
+    x_from_first,
+    x_from_second,
     rows_in,
     basis_out,
     applied_out,
@@ -511,20 +543,34 @@
     z_down, z_up = z_terms(conduct, z_index)
     low_half = lanes_of((1, LANES)) < NZ
 
-    def face_conduct(ref, at_low):
-        tile = jnp.concatenate([ref[r, ALL : ALL + 1, :] for r in range(HALF)], axis=0)
+    odd_x, odd_y = odd_lanes(ALONG_X), odd_lanes(ALONG_Y)
+
+    def y_tile(at_low, r, at):
+        one, two = y_from_first[r, at, :], y_from_second[r, at, :]
+        return jnp.where(odd_y, one, two) if at_low else jnp.where(odd_y, two, one)
+
+    def x_tile(at_low, j, at):
+        one, two = x_from_first[j, at, :], x_from_second[j, at, :]
+        return jnp.where(odd_x, one, two) if at_low else jnp.where(odd_x, two, one)
+
+    def face_conduct(at_low):
+        tile = jnp.concatenate(
+            [y_tile(at_low, r, slice(ALL, ALL + 1)) for r in range(HALF)], axis=0
+        )
         turned = pltpu.roll(tile, NZ, 1)
         pair = [tile, turned] if at_low else [turned, tile]
         return jnp.concatenate(pair, axis=0)
 
     blank = jnp.zeros((ROWS, width - LANES), F32)
-    before = jnp.concatenate([face_conduct(y_before, True), blank], axis=1)
-    after = jnp.concatenate([blank, face_conduct(y_after, False)], axis=1)
+    before = jnp.concatenate([face_conduct(True), blank], axis=1)
+    after = jnp.concatenate([blank, face_conduct(False)], axis=1)
     near_y = jnp.where(lane < NZ, before, pltpu.roll(conduct, NZ, 1))
     far_y = jnp.where(lane >= width - NZ, after, pltpu.roll(conduct, width - NZ, 1))
     x_line = [
-        jnp.concatenate([ref[j, ALL : ALL + 1, :] for j in range(CHUNKS)], axis=1)
-        for ref in (x_before, x_after)
+        jnp.concatenate(
+            [x_tile(at_low, j, slice(ALL, ALL + 1)) for j in range(CHUNKS)], axis=1
+        )
+        for at_low in (True, False)
     ]
     near_x = jnp.where(row == 0, x_line[0], pltpu.roll(conduct, 1, 0))
     far_x = jnp.where(row == ROWS - 1, x_line[1], pltpu.roll(conduct, ROWS - 1, 0))
@@ -553,13 +599,14 @@
         result = jnp.dot(weights[...], stack[...], preferred_element_type=F32)
         return result[0:NEW] + (result[NEW : 2 * NEW] + result[2 * NEW : 3 * NEW])
 
-    for ref, place in ((x_before, 0), (x_after, ROWS + 1)):
-        fill(first, [ref[j, 0:ALL, :] for j in range(CHUNKS)])
+    fields = slice(0, ALL)
+    for at_low, place in ((True, 0), (False, ROWS + 1)):
+        fill(first, [x_tile(at_low, j, fields) for j in range(CHUNKS)])
         field[place] = product(first)
-    for ref, target, at_low in ((y_before, low_y, True), (y_after, high_y, False)):
+    for target, at_low in ((low_y, True), (high_y, False)):
         for g in range(HALF // CHUNKS):
             stack = first if g % 2 == 0 else second
-            fill(stack, [ref[g * CHUNKS + j, 0:ALL, :] for j in range(CHUNKS)])
+            fill(stack, [y_tile(at_low, g * CHUNKS + j, fields) for j in range(CHUNKS)])
             value = product(stack)
             for j in range(CHUNKS):
                 tile = value[:, j * LANES : (j + 1) * LANES]
@@ -676,7 +723,7 @@
 
 
 def all_sum(block):
-    inner, outer = ("core", "z"), ("x", "y")
+    inner, outer = ("x", "y"), ("core", "z")
     piece = spread(block, inner)
     piece = jnp.sum(copies_of(piece, outer), axis=0)
     return gathered(piece, inner)
@@ -711,7 +758,7 @@
 
     tables = (conductivity, damping, drift_speed, heat_capacity)
 
-    y_top, y_low, x_top, x_low, coef = pl.pallas_call(
+    y_first, y_second, x_first, x_second, coef = pl.pallas_call(
         pack_kernel,
         grid=(1,),
         out_shape=[
@@ -740,16 +787,15 @@
         new_block,
     )
 
-    def onward(value, axis):
-        return lax.ppermute(value, axis, [(i, i + 1) for i in range(lax.axis_size(axis) - 1)])
-
-    def backward(value, axis):
-        return lax.ppermute(value, axis, [(i + 1, i) for i in range(lax.axis_size(axis) - 1)])
-
-    y_before = onward(y_top, ALONG_Y)
-    x_before = onward(x_top, ALONG_X)
-    y_after = backward(y_low, ALONG_Y)
-    x_after = backward(x_low, ALONG_X)
+    def traded(value, axes, start):
+        lower = range(start, lax.axis_size(axes) - 1, 2)
+        pairs = [(i, i + 1) for i in lower] + [(i + 1, i) for i in lower]
+        return lax.ppermute(value, axes, pairs)
+
+    y_from_first = traded(y_first, ALONG_Y, 0)
+    y_from_second = traded(y_second, ALONG_Y, 1)
+    x_from_first = traded(x_first, ALONG_X, 0)
+    x_from_second = traded(x_second, ALONG_X, 1)
 
     stack_rows = 2 * LANES + 4 * ALL
     stack_width = GROUP * CHUNKS * LANES
@@ -781,15 +827,14 @@
         ),
         name="gram",
     )(sensor_cells, coef, old_basis, new_block, source_matrix)
-    y_before, y_after, x_before, x_after, gram = lax.optimization_barrier(
-        (y_before, y_after, x_before, x_after, gram)
-    )
+    received = (y_from_first, y_from_second, x_from_first, x_from_second)
+    received, gram = lax.optimization_barrier((received, gram))
 
     face_width = (HALF + CHUNKS) * LANES
     partial = pl.pallas_call(
         face_kernel,
         out_shape=shape(PAYLOAD, LANES),
-        in_specs=[whole] * 6,
+        in_specs=[whole] * 10,
         out_specs=whole,
         scratch_shapes=[
             pltpu.VMEM((2 * ALL, face_width), BF16),
@@ -797,7 +842,7 @@
         ],
         compiler_params=params,
         name="faces",
-    )(gram, sensed, y_low, y_before, x_low, x_before)
+    )(gram, sensed, y_first, y_second, x_first, x_second, *received)
 
     summed = all_sum(partial)
 
@@ -836,10 +881,7 @@
         region_map,
         *tables,
         summed,
-        y_before,
-        y_after,
-        x_before,
-        x_after,
+        *received,
         rows,
     )
     basis, applied, stiff_block, stiff_row, capacity_block, sensor_block, source_block = results

time: 102 us -> 97.5 us (0.956)
  starting transfers between devices: 11.3 us -> 6.97 us
  blocking collectives: 44.6 us -> 42.3 us
    ppermute x4, starting transfers between devices: 11.3 us -> 6.97 us  [traded(): return lax.ppermute(value, axes, pairs)]
    all_to_all x3, blocking collectives: 44.6 us -> 42.3 us  [swap(): return lax.all_to_all(pieces, axes, 0, 0)]
  transfers between devices with their start and end apart: 4 -> 4, of which waited for: 0 -> 0; matrix products, arithmetic and copies ran while one was open for 0% -> 0% of each run, Pallas kernels for 17% -> 18%
where the time goes in v4:
time: 97.5 us; the launch traced here: 96.1 us
  Pallas kernels  44.6 us (46%)
  blocking collectives  42.3 us (43%)
  starting transfers between devices  6.97 us (7%)
  local copies, waits for them, and re-layouts  1.29 us (1%)
    all_to_all x3, blocking collectives, swap(): return lax.all_to_all(pieces, axes, 0, 0)  42.3 us
    pallas_call x1, Pallas kernels, per_device(): pl.pallas_call(functools.partial(basis_kernel, volume), out_shape=[shape(...  18 us
    pallas_call x1, Pallas kernels, per_device(): pl.pallas_call(gram_kernel, out_shape=[shape(stack_rows, 2 * LANES), shap...  17.4 us
    ppermute x4, starting transfers between devices, traded(): return lax.ppermute(value, axes, pairs)  6.97 us
    pallas_call x1, Pallas kernels, per_device(): pl.pallas_call(pack_kernel, grid=(1,), out_shape=[shape(HALF, FACE, LANES...  5.31 us
    pallas_call x1, Pallas kernels, per_device(): pl.pallas_call(face_kernel, out_shape=shape(PAYLOAD, LANES), in_specs=[wh...  3.88 us
  transfers between devices with their start and end apart: 4, of which 0 were waited for; matrix products, arithmetic and copies ran while one was open for 0% of the time, Pallas kernels for 18%

profile of v4, /device:TPU:1, one launch (start us, length us, event | category | flops | bytes accessed | tf_op | source)
XLA Modules:
  0.0 96.1 jit_solution(16332027101102767522)
XLA Ops:
  0.6 5.3 %pack.1 = (f32[16,104,128]{2,1,0:T(8,128)}, f32[16,104,128]{2,1,0:T(8,128)}, f32[4,112,128]{2,1,0:T(8,128)}, f32[4,112,128]{2,1,0:T(8,128)}, f32[32,32,128]{2,1,0:T(8,128)}) custom-call(s32[32,512]{1,0:T(8,128)} %region_ref.3, f32[8]{0:T(128)} %conductivity.3, f32[8]{0:T(128)} %damping.3, f32[8]{0:T(128)} %drift_speed.3, f32[8]{0:T(128)} %heat_capacity.3, ...), custom_call_target="tpu_custom_call" | custom-call | tf_op jit(solution)/shard_map/pack/pallas_call | solution.py:761
  5.9 2.2 %collective-permute-start = (f32[16,104,128]{2,1,0:T(8,128)}, f32[16,104,128]{2,1,0:T(8,128)S(1)}, u32[]{:S(2)}, u32[]{:S(2)}) collective-permute-start(f32[16,104,128]{2,1,0:T(8,128)} %get-tuple-element.27.y_first), channel_id=1, source_target_pairs={{0,1},{2,3},{4,5},{6,7},{8,9},{10,11},{12,13},{14,15},{16,17},{18,... | collective-permute-start | bytes 2555912 | tf_op jit(solution)/shard_map/ppermute | solution.py:793
  8.2 0.7 collective-permute-start.1
  8.9 1.2 %collective-permute-start.2 = (f32[4,112,128]{2,1,0:T(8,128)}, f32[4,112,128]{2,1,0:T(8,128)S(1)}, u32[]{:S(2)}, u32[]{:S(2)}) collective-permute-start(f32[4,112,128]{2,1,0:T(8,128)} %get-tuple-element.29.x_first), channel_id=1, source_target_pairs={{0,32},{64,96},{128,160},{192,224},{32,0},{96,64},{160,128},{224,1... | collective-permute-start | bytes 688136 | tf_op jit(solution)/shard_map/ppermute | solution.py:793
  10.1 2.8 %collective-permute-start.3 = (f32[4,112,128]{2,1,0:T(8,128)}, f32[4,112,128]{2,1,0:T(8,128)S(1)}, u32[]{:S(2)}, u32[]{:S(2)}) collective-permute-start(f32[4,112,128]{2,1,0:T(8,128)} %get-tuple-element.30.x_second), channel_id=1, source_target_pairs={{32,64},{96,128},{160,192},{64,32},{128,96},{192,160},{33,65},{97,... | collective-permute-start | bytes 688136 | tf_op jit(solution)/shard_map/ppermute | solution.py:793
  12.9 17.4 %gram.1 = (f32[640,256]{1,0:T(8,128)}, f32[96,128]{1,0:T(8,128)}, f32[32,96,512]{2,1,0:T(8,128)}) custom-call(s32[16]{0:T(128)} %sensor_cells.1, f32[32,32,128]{2,1,0:T(8,128)} %get-tuple-element.31.coef, f32[64,32,512]{2,1,0:T(8,128)} %old.3, f32[32,32,512]{2,1,0:T(8,128)} %new.3, f32[32,32,512]{2,1,0:T(8,128)} %source.1), custom_call_target="tpu_custom_call" | custom-call | flops 5368709120 | bytes 8388608 | tf_op jit(solution)/shard_map/gram/pallas_call | solution.py:802
  30.4 0.0 collective-permute-done.2.x_from_first
  30.4 0.0 copy-start.2
  30.4 0.0 collective-permute-done.3.x_from_second
  30.4 0.0 copy-start.3
  30.4 0.0 collective-permute-done.y_from_first
  30.4 0.0 copy-start
  30.4 0.0 collective-permute-done.1.y_from_second
  30.4 0.0 copy-start.1
  30.5 0.6 copy-done.2
  31.1 0.1 copy-done.3
  31.2 0.3 copy-done
  31.5 0.3 copy-done.1
  31.7 3.9 %faces.1 = f32[256,128]{1,0:T(8,128)} custom-call(f32[640,256]{1,0:T(8,128)} %get-tuple-element.33.gram, f32[96,128]{1,0:T(8,128)} %get-tuple-element.34.sensed, f32[16,104,128]{2,1,0:T(8,128)} %get-tuple-element.27.y_first, f32[16,104,128]{2,1,0:T(8,128)} %get-tuple-element.28.y_second, f32[4,112,128]{2,1,0:T(8,128)} %get-tuple-element.29.x_first, ...), custom_call_target="tpu_custom_call" | custom-call | tf_op jit(solution)/shard_map/faces/pallas_call | solution.py:834
  35.6 15.8 %all_to_all.15 = f32[16,16,128]{2,1,0:T(8,128)S(1)} all-to-all(f32[16,16,128]{2,1,0:T(8,128)} %bitcast.5), channel_id=1, replica_groups=mesh['x'=4,'core'=2,'z'=8,'y'=4] {'x','y'}, dimensions={0} | all-to-all | bytes 262144 | tf_op jit(solution)/shard_map/all_to_all | solution.py:709
  51.5 16.5 %all_to_all.16 = f32[16,16,128]{2,1,0:T(8,128)S(1)} all-to-all(f32[16,16,128]{2,1,0:T(8,128)S(1)} %broadcast_in_dim.4), channel_id=1, replica_groups=mesh['x'=4,'core'=2,'z'=8,'y'=4] {'core','z'}, dimensions={0} | all-to-all | bytes 262144 | tf_op jit(solution)/shard_map/all_to_all | solution.py:709
  68.0 9.9 %all_to_all.17 = f32[16,16,128]{2,1,0:T(8,128)} all-to-all(f32[16,16,128]{2,1,0:T(8,128)S(1)} %broadcast_in_dim.5), channel_id=1, replica_groups=mesh['x'=4,'core'=2,'z'=8,'y'=4] {'x','y'}, dimensions={0} | all-to-all | bytes 262144 | tf_op jit(solution)/shard_map/all_to_all | solution.py:709
  78.0 18.0 %basis.1 = (f32[32,32,512]{2,1,0:T(8,128)}, f32[32,32,512]{2,1,0:T(8,128)}, f32[32,96]{1,0:T(8,128)}, f32[32,64]{1,0:T(8,128)}, f32[32,96]{1,0:T(8,128)}, /*index=5*/f32[16,32]{1,0:T(8,128)}, f32[32,32]{1,0:T(8,128)}) custom-call(s32[32,512]{1,0:T(8,128)} %region_ref.3, f32[8]{0:T(128)} %conductivity.3, f32[8]{0:T(128)} %damping.3, f32[8]{0:T(128)} %drift_speed.3, ...), custom_call_target="tpu_custom_call" | custom-call | tf_op jit(solution)/shard_map/basis/pallas_call | solution.py:849
  (4 shorter events, 0.1 us)
Async XLA Ops:
  5.9 24.5 %collective-permute-start = (f32[16,104,128]{2,1,0:T(8,128)}, f32[16,104,128]{2,1,0:T(8,128)S(1)}, u32[]{:S(2)}, u32[]{:S(2)}) collective-permute-start(f32[16,104,128]{2,1,0:T(8,128)} %get-tuple-element.27.y_first), channel_id=1, source_target_pairs={{0,1},{2,3},{4,5},{6,7},{8,9},{10,11},{12,13},{14,15},{16,17},{18,... | collective-permute-start | bytes 2555912 | tf_op jit(solution)/shard_map/ppermute | solution.py:793
  8.2 22.3 %collective-permute-start.1 = (f32[16,104,128]{2,1,0:T(8,128)}, f32[16,104,128]{2,1,0:T(8,128)S(1)}, u32[]{:S(2)}, u32[]{:S(2)}) collective-permute-start(f32[16,104,128]{2,1,0:T(8,128)} %get-tuple-element.28.y_second), channel_id=1, source_target_pairs={{1,2},{3,4},{5,6},{7,8},{9,10},{11,12},{13,14},{15,16},{17,18},{19... | collective-permute-start | bytes 2555912 | tf_op jit(solution)/shard_map/ppermute | solution.py:793
  8.9 21.5 %collective-permute-start.2 = (f32[4,112,128]{2,1,0:T(8,128)}, f32[4,112,128]{2,1,0:T(8,128)S(1)}, u32[]{:S(2)}, u32[]{:S(2)}) collective-permute-start(f32[4,112,128]{2,1,0:T(8,128)} %get-tuple-element.29.x_first), channel_id=1, source_target_pairs={{0,32},{64,96},{128,160},{192,224},{32,0},{96,64},{160,128},{224,1... | collective-permute-start | bytes 688136 | tf_op jit(solution)/shard_map/ppermute | solution.py:793
  10.1 20.3 %collective-permute-start.3 = (f32[4,112,128]{2,1,0:T(8,128)}, f32[4,112,128]{2,1,0:T(8,128)S(1)}, u32[]{:S(2)}, u32[]{:S(2)}) collective-permute-start(f32[4,112,128]{2,1,0:T(8,128)} %get-tuple-element.30.x_second), channel_id=1, source_target_pairs={{32,64},{96,128},{160,192},{64,32},{128,96},{192,160},{33,65},{97,... | collective-permute-start | bytes 688136 | tf_op jit(solution)/shard_map/ppermute | solution.py:793
  30.4 0.7 copy-start.2
  30.4 0.8 copy-start.3
  30.4 1.0 %copy-start = (f32[16,104,128]{2,1,0:T(8,128)}, f32[16,104,128]{2,1,0:T(8,128)S(1)}, u32[]{:S(2)}) copy-start(f32[16,104,128]{2,1,0:T(8,128)S(1)} %collective-permute-done.y_from_first) | copy-start | bytes 2555908
  30.4 1.3 %copy-start.1 = (f32[16,104,128]{2,1,0:T(8,128)}, f32[16,104,128]{2,1,0:T(8,128)S(1)}, u32[]{:S(2)}) copy-start(f32[16,104,128]{2,1,0:T(8,128)S(1)} %collective-permute-done.1.y_from_second) | copy-start | bytes 2555908

commit v5 on v4

--- a/solution.py
+++ b/solution.py
@@ -16,7 +16,7 @@
 CHUNKS = 4
 HALF = ROWS // 2
 GROUP = 4
-PARTS = 3
+PARTS = 2
 FACE = ALL + 8
 XFACE = ALL + 16
 PAYLOAD = 2 * LANES

time: 97.5 us -> 96.1 us (0.986)
  Pallas kernels: 44.6 us -> 43.2 us
    pallas_call x1, Pallas kernels: 18 us -> 16.5 us  [per_device(): pl.pallas_call(functools.partial(basis_kernel, volume), out_shape=[shape(...]
where the time goes in v5:
time: 96.1 us; the launch traced here: 94.7 us
  Pallas kernels  43.2 us (45%)
  blocking collectives  42.3 us (44%)
  starting transfers between devices  6.97 us (7%)
  local copies, waits for them, and re-layouts  1.29 us (1%)
    all_to_all x3, blocking collectives, swap(): return lax.all_to_all(pieces, axes, 0, 0)  42.3 us
    pallas_call x1, Pallas kernels, per_device(): pl.pallas_call(gram_kernel, out_shape=[shape(stack_rows, 2 * LANES), shap...  17.4 us
    pallas_call x1, Pallas kernels, per_device(): pl.pallas_call(functools.partial(basis_kernel, volume), out_shape=[shape(...  16.5 us
    ppermute x4, starting transfers between devices, traded(): return lax.ppermute(value, axes, pairs)  6.97 us
    pallas_call x1, Pallas kernels, per_device(): pl.pallas_call(pack_kernel, grid=(1,), out_shape=[shape(HALF, FACE, LANES...  5.31 us
    pallas_call x1, Pallas kernels, per_device(): pl.pallas_call(face_kernel, out_shape=shape(PAYLOAD, LANES), in_specs=[wh...  3.88 us
  transfers between devices with their start and end apart: 4, of which 0 were waited for; matrix products, arithmetic and copies ran while one was open for 0% of the time, Pallas kernels for 18%

profile of v5, /device:TPU:1, one launch (start us, length us, event | category | flops | bytes accessed | tf_op | source)
XLA Modules:
  0.0 94.7 jit_solution(10242741228473697990)
XLA Ops:
  0.6 5.3 %pack.1 = (f32[16,104,128]{2,1,0:T(8,128)}, f32[16,104,128]{2,1,0:T(8,128)}, f32[4,112,128]{2,1,0:T(8,128)}, f32[4,112,128]{2,1,0:T(8,128)}, f32[32,32,128]{2,1,0:T(8,128)}) custom-call(s32[32,512]{1,0:T(8,128)} %region_ref.3, f32[8]{0:T(128)} %conductivity.3, f32[8]{0:T(128)} %damping.3, f32[8]{0:T(128)} %drift_speed.3, f32[8]{0:T(128)} %heat_capacity.3, ...), custom_call_target="tpu_custom_call" | custom-call | tf_op jit(solution)/shard_map/pack/pallas_call | solution.py:761
  5.9 2.2 %collective-permute-start = (f32[16,104,128]{2,1,0:T(8,128)}, f32[16,104,128]{2,1,0:T(8,128)S(1)}, u32[]{:S(2)}, u32[]{:S(2)}) collective-permute-start(f32[16,104,128]{2,1,0:T(8,128)} %get-tuple-element.27.y_first), channel_id=1, source_target_pairs={{0,1},{2,3},{4,5},{6,7},{8,9},{10,11},{12,13},{14,15},{16,17},{18,... | collective-permute-start | bytes 2555912 | tf_op jit(solution)/shard_map/ppermute | solution.py:793
  8.2 0.7 collective-permute-start.1
  8.9 1.2 %collective-permute-start.2 = (f32[4,112,128]{2,1,0:T(8,128)}, f32[4,112,128]{2,1,0:T(8,128)S(1)}, u32[]{:S(2)}, u32[]{:S(2)}) collective-permute-start(f32[4,112,128]{2,1,0:T(8,128)} %get-tuple-element.29.x_first), channel_id=1, source_target_pairs={{0,32},{64,96},{128,160},{192,224},{32,0},{96,64},{160,128},{224,1... | collective-permute-start | bytes 688136 | tf_op jit(solution)/shard_map/ppermute | solution.py:793
  10.1 2.8 %collective-permute-start.3 = (f32[4,112,128]{2,1,0:T(8,128)}, f32[4,112,128]{2,1,0:T(8,128)S(1)}, u32[]{:S(2)}, u32[]{:S(2)}) collective-permute-start(f32[4,112,128]{2,1,0:T(8,128)} %get-tuple-element.30.x_second), channel_id=1, source_target_pairs={{32,64},{96,128},{160,192},{64,32},{128,96},{192,160},{33,65},{97,... | collective-permute-start | bytes 688136 | tf_op jit(solution)/shard_map/ppermute | solution.py:793
  12.9 17.4 %gram.1 = (f32[640,256]{1,0:T(8,128)}, f32[96,128]{1,0:T(8,128)}, f32[32,96,512]{2,1,0:T(8,128)}) custom-call(s32[16]{0:T(128)} %sensor_cells.1, f32[32,32,128]{2,1,0:T(8,128)} %get-tuple-element.31.coef, f32[64,32,512]{2,1,0:T(8,128)} %old.3, f32[32,32,512]{2,1,0:T(8,128)} %new.3, f32[32,32,512]{2,1,0:T(8,128)} %source.1), custom_call_target="tpu_custom_call" | custom-call | flops 5368709120 | bytes 8388608 | tf_op jit(solution)/shard_map/gram/pallas_call | solution.py:802
  30.4 0.0 collective-permute-done.2.x_from_first
  30.4 0.0 copy-start.2
  30.4 0.0 collective-permute-done.3.x_from_second
  30.4 0.0 copy-start.3
  30.4 0.0 collective-permute-done.y_from_first
  30.4 0.0 copy-start
  30.4 0.0 collective-permute-done.1.y_from_second
  30.4 0.0 copy-start.1
  30.5 0.6 copy-done.2
  31.1 0.1 copy-done.3
  31.2 0.3 copy-done
  31.5 0.3 copy-done.1
  31.7 3.9 %faces.1 = f32[256,128]{1,0:T(8,128)} custom-call(f32[640,256]{1,0:T(8,128)} %get-tuple-element.33.gram, f32[96,128]{1,0:T(8,128)} %get-tuple-element.34.sensed, f32[16,104,128]{2,1,0:T(8,128)} %get-tuple-element.27.y_first, f32[16,104,128]{2,1,0:T(8,128)} %get-tuple-element.28.y_second, f32[4,112,128]{2,1,0:T(8,128)} %get-tuple-element.29.x_first, ...), custom_call_target="tpu_custom_call" | custom-call | tf_op jit(solution)/shard_map/faces/pallas_call | solution.py:834
  35.6 15.8 %all_to_all.15 = f32[16,16,128]{2,1,0:T(8,128)S(1)} all-to-all(f32[16,16,128]{2,1,0:T(8,128)} %bitcast.5), channel_id=1, replica_groups=mesh['x'=4,'core'=2,'z'=8,'y'=4] {'x','y'}, dimensions={0} | all-to-all | bytes 262144 | tf_op jit(solution)/shard_map/all_to_all | solution.py:709
  51.5 16.5 %all_to_all.16 = f32[16,16,128]{2,1,0:T(8,128)S(1)} all-to-all(f32[16,16,128]{2,1,0:T(8,128)S(1)} %broadcast_in_dim.4), channel_id=1, replica_groups=mesh['x'=4,'core'=2,'z'=8,'y'=4] {'core','z'}, dimensions={0} | all-to-all | bytes 262144 | tf_op jit(solution)/shard_map/all_to_all | solution.py:709
  68.0 9.9 %all_to_all.17 = f32[16,16,128]{2,1,0:T(8,128)} all-to-all(f32[16,16,128]{2,1,0:T(8,128)S(1)} %broadcast_in_dim.5), channel_id=1, replica_groups=mesh['x'=4,'core'=2,'z'=8,'y'=4] {'x','y'}, dimensions={0} | all-to-all | bytes 262144 | tf_op jit(solution)/shard_map/all_to_all | solution.py:709
  78.0 16.5 %basis.1 = (f32[32,32,512]{2,1,0:T(8,128)}, f32[32,32,512]{2,1,0:T(8,128)}, f32[32,96]{1,0:T(8,128)}, f32[32,64]{1,0:T(8,128)}, f32[32,96]{1,0:T(8,128)}, /*index=5*/f32[16,32]{1,0:T(8,128)}, f32[32,32]{1,0:T(8,128)}) custom-call(s32[32,512]{1,0:T(8,128)} %region_ref.3, f32[8]{0:T(128)} %conductivity.3, f32[8]{0:T(128)} %damping.3, f32[8]{0:T(128)} %drift_speed.3, ...), custom_call_target="tpu_custom_call" | custom-call | tf_op jit(solution)/shard_map/basis/pallas_call | solution.py:849
  (4 shorter events, 0.1 us)
Async XLA Ops:
  5.9 24.5 %collective-permute-start = (f32[16,104,128]{2,1,0:T(8,128)}, f32[16,104,128]{2,1,0:T(8,128)S(1)}, u32[]{:S(2)}, u32[]{:S(2)}) collective-permute-start(f32[16,104,128]{2,1,0:T(8,128)} %get-tuple-element.27.y_first), channel_id=1, source_target_pairs={{0,1},{2,3},{4,5},{6,7},{8,9},{10,11},{12,13},{14,15},{16,17},{18,... | collective-permute-start | bytes 2555912 | tf_op jit(solution)/shard_map/ppermute | solution.py:793
  8.2 22.3 %collective-permute-start.1 = (f32[16,104,128]{2,1,0:T(8,128)}, f32[16,104,128]{2,1,0:T(8,128)S(1)}, u32[]{:S(2)}, u32[]{:S(2)}) collective-permute-start(f32[16,104,128]{2,1,0:T(8,128)} %get-tuple-element.28.y_second), channel_id=1, source_target_pairs={{1,2},{3,4},{5,6},{7,8},{9,10},{11,12},{13,14},{15,16},{17,18},{19... | collective-permute-start | bytes 2555912 | tf_op jit(solution)/shard_map/ppermute | solution.py:793
  8.9 21.5 %collective-permute-start.2 = (f32[4,112,128]{2,1,0:T(8,128)}, f32[4,112,128]{2,1,0:T(8,128)S(1)}, u32[]{:S(2)}, u32[]{:S(2)}) collective-permute-start(f32[4,112,128]{2,1,0:T(8,128)} %get-tuple-element.29.x_first), channel_id=1, source_target_pairs={{0,32},{64,96},{128,160},{192,224},{32,0},{96,64},{160,128},{224,1... | collective-permute-start | bytes 688136 | tf_op jit(solution)/shard_map/ppermute | solution.py:793
  10.1 20.3 %collective-permute-start.3 = (f32[4,112,128]{2,1,0:T(8,128)}, f32[4,112,128]{2,1,0:T(8,128)S(1)}, u32[]{:S(2)}, u32[]{:S(2)}) collective-permute-start(f32[4,112,128]{2,1,0:T(8,128)} %get-tuple-element.30.x_second), channel_id=1, source_target_pairs={{32,64},{96,128},{160,192},{64,32},{128,96},{192,160},{33,65},{97,... | collective-permute-start | bytes 688136 | tf_op jit(solution)/shard_map/ppermute | solution.py:793
  30.4 0.7 copy-start.2
  30.4 0.8 copy-start.3
  30.4 1.0 %copy-start = (f32[16,104,128]{2,1,0:T(8,128)}, f32[16,104,128]{2,1,0:T(8,128)S(1)}, u32[]{:S(2)}) copy-start(f32[16,104,128]{2,1,0:T(8,128)S(1)} %collective-permute-done.y_from_first) | copy-start | bytes 2555908
  30.4 1.3 %copy-start.1 = (f32[16,104,128]{2,1,0:T(8,128)}, f32[16,104,128]{2,1,0:T(8,128)S(1)}, u32[]{:S(2)}) copy-start(f32[16,104,128]{2,1,0:T(8,128)S(1)} %collective-permute-done.1.y_from_second) | copy-start | bytes 2555908
